TPU v7x, 512 devices: a whole 4x4x16 slice. The times are simulated.
512 devices in a mesh: clus: 128 (over z, x, core), sk: 4 (over y).
Axes of the slice: x: 4, y: 4, z: 16, core: 2. Of those that a mesh axis runs over, the one named last changes fastest.
Arguments:
- positions: float32 [3, 1048576], P(None, 'clus'), as said below
- sketch: bfloat16 [256, 1048576], P('sk', 'clus'), may hold values from -24 to 24
- near: int32 [4096, 9], P('clus'), may hold values from 0 to 1, as said below
Outputs:
- sketch_image: float32 [256, 1048576], P('sk', 'clus')
- node_factor: float32 [32768, 256], P('clus', 'sk')
- pair_factor: float32 [32768, 256], P('clus', 'sk')
- group_factor: float32 [32768, 256], P('clus', 'sk')
Inputs may be any that keep to these rules, and one draw needn't show every extreme that they name: `positions`: column i is the position of point i, which belongs to cluster i // 256. Along the first coordinate each cluster occupies an interval of its own; these intervals do not intersect, and a cluster with a larger index lies entirely at larger first coordinates than one with a smaller index. The second and third coordinates lie in [0, 1). near[c, 4 + d] is 1 where cluster c + d exists and lies in the near field of cluster c, else 0; columns 3, 4 and 5 are 1 wherever that cluster exists; the relation is symmetric: near[c, 4 + d] = near[c + d, 4 - d].
All inputs are finite; a program needn't handle non-finite values.
Results may differ from a plain program's by a relative error of at most 0.00057.
Values may be sent and summed in bfloat16 or wider, within the bound.
No kernel may reach another device: no remote copies, remote signals or barrier semaphores. Data moves between devices by JAX's collectives and lax.ppermute only.
A program may use at most 128 MiB of HBM per device.

v0:
```python
import math

import jax
import jax.numpy as jnp
from jax import lax
from jax.experimental import pallas as pl
from jax.experimental.pallas import tpu as pltpu
from jax.sharding import Mesh
from jax.sharding import PartitionSpec as P

CS = 256
H = 4
MIB = 2**20
RATE = math.sqrt(3.0) / 0.3
NUGGET = 1.0
FAMILY = 4
UNROLL = 4
PANEL = 16
SHIFT = 64


def near_field_kernel(pos, sk, low, high, near, image, rounded, across, along, cols, acc, todo):
    slices, rows = sk.shape
    own = rows // CS
    last = own + 2 * H

    def joined(block):
        parts = [block[slices + r : slices + r + 1, :].astype(jnp.float32) for r in range(9)]
        return jnp.concatenate([parts[r] + parts[r + 1] + parts[r + 2] for r in (0, 3, 6)], axis=0)

    for slot in range(last):
        if slot < H:
            a = slot * CS
            block, p = low[:slices, a : a + CS], joined(low[:, a : a + CS])
        elif slot < H + own:
            a = (slot - H) * CS
            block, p = sk[:, a : a + CS], pos[:, a : a + CS]
        else:
            a = (slot - H - own) * CS
            block, p = high[:slices, a : a + CS], joined(high[:, a : a + CS])
        cols[slot] = block
        for r in range(3):
            along[slot, :, r * 128 : (r + 1) * 128] = jnp.broadcast_to(p[r : r + 1, :], (128, CS)).T
        across[slot] = p
        acc[slot] = jnp.zeros((slices, CS), jnp.float32)
    cols[last] = jnp.zeros((slices, CS), jnp.bfloat16)
    along[last] = jnp.zeros((CS, 384), jnp.float32)
    across[last] = jnp.zeros((3, CS), jnp.float32)

    def tile(c, s):
        squared = 1e-30
        for r in range(3):
            point = along[s, :, r * 128 : (r + 1) * 128]
            diff = jnp.concatenate([point, point], axis=1) - across[c, r : r + 1]
            squared = squared + diff * diff
        dist = squared * lax.rsqrt(squared)
        return ((1.0 + RATE * dist) * jnp.exp2(dist * (-RATE * math.log2(math.e)))).astype(jnp.bfloat16)

    def forward(s, t):
        return jnp.dot(cols[s], t, preferred_element_type=jnp.float32)

    def backward(c, t):
        return lax.dot_general(cols[c], t, (((1,), (1,)), ((), ())), preferred_element_type=jnp.float32)

    count = jnp.int32(0)
    for s in range(H):
        for d in range(s + 1, H + 1):
            todo[count] = (s - d + H) * SHIFT + s + H
            count = count + near[s, H - d]

    def close_step(i, count):
        results = []
        for u in range(2):
            c = i * 2 + u
            for d in range(2, H + 1):
                todo[count] = (c + H) * SHIFT + c + d + H
                count = count + near[c, H + d]
            c = c + H
            same, next_one = tile(c, c), tile(c, c + 1)
            results.append((c, forward(c, same) + forward(c + 1, next_one), backward(c, next_one)))
        for c, here, there in results:
            acc[c] = acc[c] + here
            acc[c + 1] = acc[c + 1] + there
        return count

    count = lax.fori_loop(0, own // 2, close_step, count)
    for i in range(UNROLL):
        todo[count + i] = last * (SHIFT + 1)

    def far_step(i, carry):
        results = []
        for u in range(UNROLL):
            code = todo[i * UNROLL + u]
            c, s = code // SHIFT, code % SHIFT
            t = tile(c, s)
            results.append((c, s, forward(s, t), backward(c, t)))
        for c, s, here, there in results:
            acc[c] = acc[c] + here
            acc[s] = acc[s] + there
        return carry

    lax.fori_loop(0, (count + UNROLL - 1) // UNROLL, far_step, 0)

    per = own // rounded.shape[0]
    for c in range(own):
        value = acc[c + H] * (8.0 / CS) + NUGGET * cols[c + H].astype(jnp.float32)
        image[:, c * CS : (c + 1) * CS] = value
        rounded[c // per, :, (c % per) * CS : (c % per + 1) * CS] = value.astype(jnp.bfloat16)


def near_field(pos, sk, low, high, near, shares):
    slices, rows = sk.shape
    slots = rows // CS + 2 * H + 1
    whole = pl.BlockSpec(memory_space=pltpu.VMEM)
    return pl.pallas_call(
        near_field_kernel,
        out_shape=(
            jax.ShapeDtypeStruct((slices, rows), jnp.float32),
            jax.ShapeDtypeStruct((shares, slices, rows // shares), jnp.bfloat16),
        ),
        in_specs=[whole, whole, whole, whole, pl.BlockSpec(memory_space=pltpu.SMEM)],
        out_specs=(whole, whole),
        scratch_shapes=[
            pltpu.VMEM((slots, 3, CS), jnp.float32),
            pltpu.VMEM((slots, CS, 3 * 128), jnp.float32),
            pltpu.VMEM((slots, slices, CS), jnp.bfloat16),
            pltpu.VMEM((slots, slices, CS), jnp.float32),
            pltpu.SMEM((slots * H + 2 * UNROLL,), jnp.int32),
        ],
        compiler_params=pltpu.CompilerParams(vmem_limit_bytes=36 * MIB),
        name="near_field",
    )(pos, sk, low, high, near)


def gram_kernel(points, out, *, scale):
    whole = points[...].reshape(-1, points.shape[-1])
    half = whole.shape[0] // 2
    product = lax.dot_general(whole, whole, (((1,), (1,)), ((), ())), preferred_element_type=jnp.float32) * scale
    out[:half] = product[:half, :half]
    out[half : 2 * half] = product[:half, half:]
    out[2 * half :] = product[half:, half:]


def partial_gram(points, scale):
    half = points.shape[0] * points.shape[1] // 2
    return pl.pallas_call(
        lambda points, out: gram_kernel(points, out, scale=scale),
        out_shape=jax.ShapeDtypeStruct((3 * half, half), jnp.float32),
        compiler_params=pltpu.CompilerParams(vmem_limit_bytes=32 * MIB),
        name="partial_gram",
    )(points)


def combine_kernel(parts, out):
    k, s = out.shape[0], out.shape[1]
    nodes = []
    for i in range(k):
        total = parts[i * s]
        for j in range(1, s):
            total = total + parts[i * s + j]
        nodes.append(total)
    pairs = [(nodes[i] + nodes[i + 1]) * 0.5 for i in range(0, k, 2)]
    group = (pairs[0] + pairs[1]) * 0.5
    for i in range(k):
        for j in range(s):
            out[i, j, 0] = nodes[i]
            out[i, j, 1] = pairs[i // 2]
            out[i, j, 2] = group


def combine(parts, k, s):
    return pl.pallas_call(
        combine_kernel,
        out_shape=jax.ShapeDtypeStruct((k, s, 3) + parts.shape[1:], jnp.float32),
        name="combine",
    )(parts)


def pieces(value):
    high = value.astype(jnp.bfloat16)
    rest = value - high.astype(jnp.float32)
    mid = rest.astype(jnp.bfloat16)
    low = (rest - mid.astype(jnp.float32)).astype(jnp.bfloat16)
    return high, mid, low


def cholesky_kernel(place, slabs, first, second, third, work, upper):
    sources, mats, depth, half = slabs.shape
    n = 2 * half
    for j in range(sources):
        for t in range(0, depth, 8):
            row = j * depth + t
            block, at = row // half, row % half
            for m in range(mats):
                value = slabs[j, m, t : t + 8]
                if block < 2:
                    work[m, at : at + 8, block * half : (block + 1) * half] = value
                else:
                    work[m, half + at : half + at + 8, half:] = value
    for m in range(mats):
        upper[m, half:, :half] = jnp.zeros((half, half), jnp.float32)
    rowid = lax.broadcasted_iota(jnp.int32, (8, 128), 0)
    spread = lambda row: jnp.broadcast_to(row, (8, 128))
    for j0 in range(0, n, PANEL):
        lane0 = 0 if j0 < half else half
        width = (n - lane0) // 128
        rows, cols, scale = [], [], []
        for m in range(mats):
            block = work[m, j0 : j0 + PANEL, lane0:]
            rows.append(
                [[block[8 * h : 8 * h + 8, 128 * w : 128 * w + 128] for w in range(width)] for h in range(2)]
            )
            at = j0 - lane0
            cols.append(
                [[spread(block[8 * h : 8 * h + 8, at + c : at + c + 1]) for h in range(2)] for c in range(PANEL)]
            )
            scale.append([jnp.zeros((8, 128), jnp.float32) for h in range(2)])
        for q in range(PANEL):
            hq, r = q // 8, q % 8
            for m in range(mats):
                inv = lax.rsqrt(spread(cols[m][q][hq][r : r + 1, :]))
                scale[m][hq] = jnp.where(rowid == r, inv, scale[m][hq])
                inv2 = inv * inv
                factor = [None, None]
                for h in range(hq, 2):
                    f = cols[m][q][h] * inv2
                    factor[h] = jnp.where(rowid > r, f, 0.0) if h == hq else f
                for c in range(q + 1, PANEL):
                    row = spread(cols[m][c][hq][r : r + 1, :])
                    for h in range(hq, 2):
                        cols[m][c][h] = cols[m][c][h] - factor[h] * row
                for w in range(width):
                    row = spread(rows[m][hq][w][r : r + 1, :])
                    for h in range(hq, 2):
                        rows[m][h][w] = rows[m][h][w] - factor[h] * row
        for m in range(mats):
            done = jnp.concatenate(
                [
                    jnp.concatenate([rows[m][h][w] * scale[m][h] for w in range(width)], axis=1)
                    for h in range(2)
                ],
                axis=0,
            )
            upper[m, j0 : j0 + PANEL, lane0:] = done
            start = j0 + PANEL
            if start < n:
                high, mid, low = pieces(done)
                skip = (0 if start < half else half) - lane0
                left = jnp.concatenate([high, high, mid, high, mid, low], axis=0)[:, skip:]
                right = jnp.concatenate([high, mid, high, low, mid, high], axis=0)[:, skip:]
                product = lax.dot_general(left, right, (((0,), (0,)), ((), ())), preferred_element_type=jnp.float32)
                if start < half:
                    work[m, start:half, :] = work[m, start:half, :] - product[start:half, :]
                    work[m, half:, half:] = work[m, half:, half:] - product[half:, half:]
                else:
                    work[m, start:, half:] = work[m, start:, half:] - product[start - half :, :]
    wide = first.shape[1]
    begin = pl.multiple_of(place[0] * wide, wide)
    i = lax.broadcasted_iota(jnp.int32, (wide, n), 0) + begin
    j = lax.broadcasted_iota(jnp.int32, (wide, n), 1)
    for m, out in enumerate((first, second, third)):
        out[...] = jnp.where(j >= i, upper[m, pl.ds(begin, wide), :], 0.0).T


def cholesky(place, slabs, wide):
    half = slabs.shape[3]
    whole = pl.BlockSpec(memory_space=pltpu.VMEM)
    return pl.pallas_call(
        cholesky_kernel,
        out_shape=(jax.ShapeDtypeStruct((2 * half, wide), jnp.float32),) * 3,
        in_specs=[pl.BlockSpec(memory_space=pltpu.SMEM), whole],
        out_specs=(whole,) * 3,
        scratch_shapes=[pltpu.VMEM((3, 2 * half, 2 * half), jnp.float32)] * 2,
        compiler_params=pltpu.CompilerParams(vmem_limit_bytes=32 * MIB),
        name="cholesky",
    )(place, slabs)


def edge(positions, sketch):
    high = lax.reduce_precision(positions, 8, 7)
    rest = positions - high
    mid = lax.reduce_precision(rest, 8, 7)
    parts = jnp.stack([high, mid, rest - mid], axis=1).reshape(9, -1).astype(jnp.bfloat16)
    return jnp.concatenate([sketch, jnp.pad(parts, ((0, 7), (0, 0)))], axis=0)


def on_device(positions, sketch, near):
    slices, rows = sketch.shape
    margin = H * CS
    clus = ("tree", "child")
    count = lax.axis_size(clus)
    shares = lax.axis_size("sk")
    forward = [(i, i + 1) for i in range(count - 1)]
    backward = [(i + 1, i) for i in range(count - 1)]
    low = lax.ppermute(edge(positions[:, -margin:], sketch[:, -margin:]), clus, forward)
    high = lax.ppermute(edge(positions[:, :margin], sketch[:, :margin]), clus, backward)
    image, rounded = near_field(positions, sketch, low, high, near, shares)
    traded = lax.all_to_all(rounded, "sk", split_axis=0, concat_axis=0, tiled=True)
    gram = partial_gram(traded, 1.0 / rows)
    family = FAMILY * shares
    slab = gram.reshape(family, -1, gram.shape[1])
    parts = lax.all_to_all(slab, ("child", "sk"), split_axis=0, concat_axis=0, tiled=True)
    sums = combine(parts, FAMILY, shares)
    sums = sums.reshape(family, 3 * slab.shape[1], slab.shape[2])
    slabs = lax.all_to_all(sums, ("child", "sk"), split_axis=0, concat_axis=0, tiled=True)
    slabs = slabs.reshape(family, 3, slab.shape[1], slab.shape[2])
    place = lax.axis_index("sk").astype(jnp.int32).reshape(1)
    return (image, *cholesky(place, slabs, slices))


def solution(mesh):
    clusters, shares = mesh.devices.shape
    split = Mesh(mesh.devices.reshape(clusters // FAMILY, FAMILY, shares), ("tree", "child", "sk"))
    clus = ("tree", "child")
    return jax.shard_map(
        on_device,
        mesh=split,
        in_specs=(P(None, clus), P("sk", clus), P(clus, None)),
        out_specs=(P("sk", clus), P(clus, "sk"), P(clus, "sk"), P(clus, "sk")),
        check_vma=False,
    )
```

profile of v0, /device:TPU:129, one launch (start us, length us, event | category | flops | bytes accessed | tf_op | source)
XLA Modules:
  0.0 99.7 jit_solution(6894950312152218026)
XLA Ops:
  0.6 0.0 copy-start
  0.6 0.8 fusion.8
  1.6 1.0 fusion.12
  2.6 3.7 %collective-permute-start = (bf16[80,1024]{1,0:T(8,128)(2,1)S(1)}, bf16[80,1024]{1,0:T(8,128)(2,1)S(1)}, u32[]{:S(2)}, u32[]{:S(2)}) collective-permute-start(bf16[80,1024]{1,0:T(8,128)(2,1)S(1)} %fusion.2), channel_id=1, source_target_pairs={{0,4},{4,8},{8,12},{12,16},{16,20},{20,24},{24,28},{28,32},{32,36}... | collective-permute-start | bytes 491528 | tf_op jit(solution)/shard_map/ppermute | solution.py:295
  6.4 1.9 %collective-permute-start.1 = (bf16[80,1024]{1,0:T(8,128)(2,1)S(1)}, bf16[80,1024]{1,0:T(8,128)(2,1)S(1)}, u32[]{:S(2)}, u32[]{:S(2)}) collective-permute-start(bf16[80,1024]{1,0:T(8,128)(2,1)S(1)} %fusion.3), channel_id=1, source_target_pairs={{4,0},{8,4},{12,8},{16,12},{20,16},{24,20},{28,24},{32,28},{36,32}... | collective-permute-start | bytes 491528 | tf_op jit(solution)/shard_map/ppermute | solution.py:296
  8.3 0.8 copy.9.near
  9.1 0.0 collective-permute-done.low
  9.1 3.9 %collective-permute-done.1.high = bf16[80,1024]{1,0:T(8,128)(2,1)S(1)} collective-permute-done((bf16[80,1024]{1,0:T(8,128)(2,1)S(1)}, bf16[80,1024]{1,0:T(8,128)(2,1)S(1)}, u32[]{:S(2)}, u32[]{:S(2)}) %collective-permute-start.1) | collective-permute-done | bytes 163872 | tf_op jit(solution)/shard_map/ppermute | solution.py:296
  13.0 0.0 copy-done
  13.0 0.0 copy-start.1
  13.0 0.9 copy-done.1
  13.9 26.1 %near_field.1 = (f32[64,8192]{1,0:T(8,128)}, bf16[4,64,2048]{2,1,0:T(8,128)(2,1)S(1)}) custom-call(f32[3,8192]{1,0:T(4,128)S(1)} %copy-done.1, bf16[64,8192]{1,0:T(8,128)(2,1)S(1)} %copy-done, bf16[80,1024]{1,0:T(8,128)(2,1)S(1)} %collective-permute-done.low, bf16[80,1024]{1,0:T(8,128)(2,1)S(1)} %collective-permute-done.1.high, s32[32,9]{1,0:T(8,128)S(1)} %copy.9.near), custom_call_target="tpu_custom_call" | custom-call | tf_op jit(solution)/shard_map/near_field/pallas_call | solution.py:115
  40.0 17.5 %all_to_all.15.points = bf16[4,64,2048]{2,1,0:T(8,128)(2,1)S(1)} all-to-all(bf16[4,64,2048]{2,1,0:T(8,128)(2,1)S(1)} %get-tuple-element.10), channel_id=1, replica_groups=mesh['tree'=32,'child'=4,'sk'=4] {'sk'}, dimensions={0} | all-to-all | bytes 2097152 | tf_op jit(solution)/shard_map/all_to_all | solution.py:298
  57.5 0.5 partial_gram.1
  58.0 12.6 %all_to_all.16.parts = f32[16,24,128]{2,1,0:T(8,128)} all-to-all(f32[16,24,128]{2,1,0:T(8,128)S(1)} %bitcast.17), channel_id=1, replica_groups=mesh['tree'=32,'child'=4,'sk'=4] {'child','sk'}, dimensions={0} | all-to-all | bytes 393216 | tf_op jit(solution)/shard_map/all_to_all | solution.py:302
  70.5 1.8 %combine.1 = f32[4,4,3,24,128]{4,3,2,1,0:T(8,128)} custom-call(f32[16,24,128]{2,1,0:T(8,128)} %all_to_all.16.parts), custom_call_target="tpu_custom_call" | custom-call | tf_op jit(solution)/shard_map/combine/pallas_call | solution.py:172
  72.3 3.8 %all-to-all-start.2 = ((f32[16,72,128]{2,1,0:T(8,128)}), f32[16,72,128]{2,1,0:T(8,128)S(1)}, u32[]{:S(2)}, u32[]{:S(2)}) async-start(f32[16,72,128]{2,1,0:T(8,128)} %bitcast.18), calls=%async_computation.2 | async-start | bytes 1179648 | tf_op jit(solution)/shard_map/all_to_all | solution.py:305
  76.2 10.9 %all-to-all-done.2 = f32[16,72,128]{2,1,0:T(8,128)S(1)} async-done(((f32[16,72,128]{2,1,0:T(8,128)}), f32[16,72,128]{2,1,0:T(8,128)S(1)}, u32[]{:S(2)}, u32[]{:S(2)}) %all-to-all-start.2) | async-done | bytes 589856 | tf_op jit(solution)/shard_map/all_to_all | solution.py:305
  87.1 10.5 %cholesky.1 = (f32[256,64]{1,0:T(8,128)S(1)}, f32[256,64]{1,0:T(8,128)S(1)}, f32[256,64]{1,0:T(8,128)S(1)}) custom-call(s32[1]{0:T(128)} %bitcast.6.place, f32[16,3,24,128]{3,2,1,0:T(8,128)S(1)} %bitcast.16), custom_call_target="tpu_custom_call" | custom-call | tf_op jit(solution)/shard_map/cholesky/pallas_call | solution.py:268
  97.6 0.7 copy.10
  98.3 0.7 copy.11
  99.0 0.7 copy.12
  (7 shorter events, 0.2 us)
Async XLA Ops:
  0.6 12.4 %copy-start = (bf16[64,8192]{1,0:T(8,128)(2,1)S(1)}, bf16[64,8192]{1,0:T(8,128)(2,1)}, u32[]{:S(2)}) copy-start(bf16[64,8192]{1,0:T(8,128)(2,1)} %sk.1) | copy-start | bytes 3145732
  2.6 6.5 %collective-permute-start = (bf16[80,1024]{1,0:T(8,128)(2,1)S(1)}, bf16[80,1024]{1,0:T(8,128)(2,1)S(1)}, u32[]{:S(2)}, u32[]{:S(2)}) collective-permute-start(bf16[80,1024]{1,0:T(8,128)(2,1)S(1)} %fusion.2), channel_id=1, source_target_pairs={{0,4},{4,8},{8,12},{12,16},{16,20},{20,24},{24,28},{28,32},{32,36}... | collective-permute-start | bytes 491528 | tf_op jit(solution)/shard_map/ppermute | solution.py:295
  6.4 6.6 %collective-permute-start.1 = (bf16[80,1024]{1,0:T(8,128)(2,1)S(1)}, bf16[80,1024]{1,0:T(8,128)(2,1)S(1)}, u32[]{:S(2)}, u32[]{:S(2)}) collective-permute-start(bf16[80,1024]{1,0:T(8,128)(2,1)S(1)} %fusion.3), channel_id=1, source_target_pairs={{4,0},{8,4},{12,8},{16,12},{20,16},{24,20},{28,24},{32,28},{36,32}... | collective-permute-start | bytes 491528 | tf_op jit(solution)/shard_map/ppermute | solution.py:296
  13.0 0.9 copy-start.1
  72.3 14.7 %all-to-all-start.2 = ((f32[16,72,128]{2,1,0:T(8,128)}), f32[16,72,128]{2,1,0:T(8,128)S(1)}, u32[]{:S(2)}, u32[]{:S(2)}) async-start(f32[16,72,128]{2,1,0:T(8,128)} %bitcast.18), calls=%async_computation.2 | async-start | bytes 1179648 | tf_op jit(solution)/shard_map/all_to_all | solution.py:305
where the time goes:
time: 100 us; the launch traced here: 99.7 us
  Pallas kernels  38.8 us (39%)
  blocking collectives  30.1 us (30%)
  waiting for transfers between devices  14.9 us (15%)
  starting transfers between devices  9.42 us (9%)
  local copies, waits for them, and re-layouts  4.91 us (5%)
    pallas_call x1, Pallas kernels, near_field(): pl.pallas_call(near_field_kernel, out_shape=(jax.ShapeDtypeStruct((slices...  26.1 us
    all_to_all x1, blocking collectives, on_device(): lax.all_to_all(rounded, 'sk', split_axis=0, concat_axis=0, tiled=True)  17.5 us
    all_to_all x1, blocking collectives, on_device(): lax.all_to_all(slab, ('child', 'sk'), split_axis=0, concat_axis=0, tiled=...  12.6 us
    all_to_all x1, waiting for transfers between devices, on_device(): lax.all_to_all(sums, ('child', 'sk'), split_axis=0, concat_axis=0, tiled=...  10.9 us
    pallas_call x1, Pallas kernels, cholesky(): pl.pallas_call(cholesky_kernel, out_shape=(jax.ShapeDtypeStruct((2 * half...  10.5 us
    ppermute x1, waiting for transfers between devices, on_device(): lax.ppermute(edge(positions[:, :margin], sketch[:, :margin]), clus, backw...  3.93 us
    unnamed x8, local copies, waits for them, and re-layouts  3.83 us
    all_to_all x1, starting transfers between devices, on_device(): lax.all_to_all(sums, ('child', 'sk'), split_axis=0, concat_axis=0, tiled=...  3.82 us
  transfers between devices with their start and end apart: 3, of which 2 were waited for; matrix products, arithmetic and copies ran while one was open for 1% of the time, Pallas kernels for 0%

commit v1 on v0

--- a/solution.py
+++ b/solution.py
@@ -19,14 +19,19 @@
 SHIFT = 64
 
 
-def near_field_kernel(pos, sk, low, high, near, image, rounded, across, along, cols, acc, todo):
+def near_field_kernel(pos, sk, low, high, near, image, rounded, across, along, cols, acc, held, todo):
     slices, rows = sk.shape
     own = rows // CS
+    half = CS // 2
     last = own + 2 * H
 
     def joined(block):
         parts = [block[slices + r : slices + r + 1, :].astype(jnp.float32) for r in range(9)]
         return jnp.concatenate([parts[r] + parts[r + 1] + parts[r + 2] for r in (0, 3, 6)], axis=0)
+
+    def copy_along(slot):
+        for r in range(3):
+            along[slot, :, r * 128 : (r + 1) * 128] = jnp.broadcast_to(across[slot, r : r + 1], (128, CS)).T
 
     for slot in range(last):
         if slot < H:
@@ -39,67 +44,94 @@
             a = (slot - H - own) * CS
             block, p = high[:slices, a : a + CS], joined(high[:, a : a + CS])
         cols[slot] = block
-        for r in range(3):
-            along[slot, :, r * 128 : (r + 1) * 128] = jnp.broadcast_to(p[r : r + 1, :], (128, CS)).T
         across[slot] = p
         acc[slot] = jnp.zeros((slices, CS), jnp.float32)
     cols[last] = jnp.zeros((slices, CS), jnp.bfloat16)
     along[last] = jnp.zeros((CS, 384), jnp.float32)
     across[last] = jnp.zeros((3, CS), jnp.float32)
-
-    def tile(c, s):
+    for slot in range(H, H + 3):
+        copy_along(slot)
+    for slot in range(H + own, last):
+        copy_along(slot)
+
+    def tile(c, s, i=0, j=0, size=CS):
         squared = 1e-30
         for r in range(3):
-            point = along[s, :, r * 128 : (r + 1) * 128]
-            diff = jnp.concatenate([point, point], axis=1) - across[c, r : r + 1]
+            point = along[s, i : i + size, r * 128 : (r + 1) * 128]
+            if size > 128:
+                point = jnp.concatenate([point, point], axis=1)
+            diff = point - across[c, r : r + 1, j : j + size]
             squared = squared + diff * diff
         dist = squared * lax.rsqrt(squared)
         return ((1.0 + RATE * dist) * jnp.exp2(dist * (-RATE * math.log2(math.e)))).astype(jnp.bfloat16)
 
-    def forward(s, t):
-        return jnp.dot(cols[s], t, preferred_element_type=jnp.float32)
-
-    def backward(c, t):
-        return lax.dot_general(cols[c], t, (((1,), (1,)), ((), ())), preferred_element_type=jnp.float32)
-
-    count = jnp.int32(0)
+    def product(x, t):
+        return jnp.dot(x, t, preferred_element_type=jnp.float32)
+
+    def product_t(x, t):
+        return lax.dot_general(x, t, (((1,), (1,)), ((), ())), preferred_element_type=jnp.float32)
+
+    count = jnp.int32(UNROLL)
     for s in range(H):
         for d in range(s + 1, H + 1):
             todo[count] = (s - d + H) * SHIFT + s + H
-            count = count + near[s, H - d]
+            count = count + near[H - d, s]
+
+    def close_products(c, buf):
+        x = cols[c]
+        t = held[buf + 1]
+        ahead = product(cols[c + 1], t)
+        acc[c] = acc[c] + (product(x, held[buf]) + ahead)
+        acc[c + 1] = acc[c + 1] + product_t(x, t)
+
+    def close_tiles(c, buf):
+        held[buf, :half, :half] = tile(c, c, 0, 0, half)
+        corner = tile(c, c, 0, half, half)
+        held[buf, :half, half:] = corner
+        held[buf, half:, :half] = corner.T
+        held[buf, half:, half:] = tile(c, c, half, half, half)
+        held[buf + 1] = tile(c, c + 1)
 
     def close_step(i, count):
-        results = []
+        c = i * 2 + H
         for u in range(2):
-            c = i * 2 + u
+            close_products(c - 2 + u, 2 * u)
+        for u in range(2):
             for d in range(2, H + 1):
-                todo[count] = (c + H) * SHIFT + c + d + H
-                count = count + near[c, H + d]
-            c = c + H
-            same, next_one = tile(c, c), tile(c, c + 1)
-            results.append((c, forward(c, same) + forward(c + 1, next_one), backward(c, next_one)))
-        for c, here, there in results:
-            acc[c] = acc[c] + here
-            acc[c + 1] = acc[c + 1] + there
+                todo[count] = (c + u) * SHIFT + c + u + d
+                count = count + near[H + d, c + u - H]
+            copy_along(c + u + 3)
+            close_tiles(c + u, 2 * u)
         return count
 
+    held[...] = jnp.zeros(held.shape, jnp.bfloat16)
     count = lax.fori_loop(0, own // 2, close_step, count)
+    for u in range(2):
+        close_products(H + own - 2 + u, 2 * u)
+    for slot in range(H):
+        copy_along(slot)
     for i in range(UNROLL):
+        todo[i] = last * (SHIFT + 1)
         todo[count + i] = last * (SHIFT + 1)
 
-    def far_step(i, carry):
-        results = []
+    def far_products(i):
         for u in range(UNROLL):
             code = todo[i * UNROLL + u]
             c, s = code // SHIFT, code % SHIFT
-            t = tile(c, s)
-            results.append((c, s, forward(s, t), backward(c, t)))
-        for c, s, here, there in results:
-            acc[c] = acc[c] + here
-            acc[s] = acc[s] + there
+            t = held[u]
+            acc[c] = acc[c] + product(cols[s], t)
+            acc[s] = acc[s] + product_t(cols[c], t)
+
+    def far_step(i, carry):
+        far_products(i - 1)
+        for u in range(UNROLL):
+            code = todo[i * UNROLL + u]
+            held[u] = tile(code // SHIFT, code % SHIFT)
         return carry
 
-    lax.fori_loop(0, (count + UNROLL - 1) // UNROLL, far_step, 0)
+    steps = (count + UNROLL - 1) // UNROLL
+    lax.fori_loop(1, steps, far_step, 0)
+    far_products(steps - 1)
 
     per = own // rounded.shape[0]
     for c in range(own):
@@ -125,7 +157,8 @@
             pltpu.VMEM((slots, CS, 3 * 128), jnp.float32),
             pltpu.VMEM((slots, slices, CS), jnp.bfloat16),
             pltpu.VMEM((slots, slices, CS), jnp.float32),
-            pltpu.SMEM((slots * H + 2 * UNROLL,), jnp.int32),
+            pltpu.VMEM((UNROLL, CS, CS), jnp.bfloat16),
+            pltpu.SMEM((slots * H + 4 * UNROLL,), jnp.int32),
         ],
         compiler_params=pltpu.CompilerParams(vmem_limit_bytes=36 * MIB),
         name="near_field",
@@ -254,12 +287,12 @@
                     work[m, half:, half:] = work[m, half:, half:] - product[half:, half:]
                 else:
                     work[m, start:, half:] = work[m, start:, half:] - product[start - half :, :]
-    wide = first.shape[1]
+    wide = first.shape[0]
     begin = pl.multiple_of(place[0] * wide, wide)
     i = lax.broadcasted_iota(jnp.int32, (wide, n), 0) + begin
     j = lax.broadcasted_iota(jnp.int32, (wide, n), 1)
     for m, out in enumerate((first, second, third)):
-        out[...] = jnp.where(j >= i, upper[m, pl.ds(begin, wide), :], 0.0).T
+        out[...] = jnp.where(j >= i, upper[m, pl.ds(begin, wide), :], 0.0)
 
 
 def cholesky(place, slabs, wide):
@@ -267,7 +300,7 @@
     whole = pl.BlockSpec(memory_space=pltpu.VMEM)
     return pl.pallas_call(
         cholesky_kernel,
-        out_shape=(jax.ShapeDtypeStruct((2 * half, wide), jnp.float32),) * 3,
+        out_shape=(jax.ShapeDtypeStruct((wide, 2 * half), jnp.float32),) * 3,
         in_specs=[pl.BlockSpec(memory_space=pltpu.SMEM), whole],
         out_specs=(whole,) * 3,
         scratch_shapes=[pltpu.VMEM((3, 2 * half, 2 * half), jnp.float32)] * 2,
@@ -294,7 +327,7 @@
     backward = [(i + 1, i) for i in range(count - 1)]
     low = lax.ppermute(edge(positions[:, -margin:], sketch[:, -margin:]), clus, forward)
     high = lax.ppermute(edge(positions[:, :margin], sketch[:, :margin]), clus, backward)
-    image, rounded = near_field(positions, sketch, low, high, near, shares)
+    image, rounded = near_field(positions, sketch, low, high, near.T, shares)
     traded = lax.all_to_all(rounded, "sk", split_axis=0, concat_axis=0, tiled=True)
     gram = partial_gram(traded, 1.0 / rows)
     family = FAMILY * shares
@@ -305,7 +338,7 @@
     slabs = lax.all_to_all(sums, ("child", "sk"), split_axis=0, concat_axis=0, tiled=True)
     slabs = slabs.reshape(family, 3, slab.shape[1], slab.shape[2])
     place = lax.axis_index("sk").astype(jnp.int32).reshape(1)
-    return (image, *cholesky(place, slabs, slices))
+    return (image, *(factor.T for factor in cholesky(place, slabs, slices)))
 
 
 def solution(mesh):

time: 100 us -> 96.1 us (0.961)
  the two profiles are of different devices: /device:TPU:129 before, /device:TPU:161 now
where the time goes in v1:
time: 96.1 us; the launch traced here: 95.7 us
  Pallas kernels  36.3 us (38%)
  blocking collectives  30.1 us (31%)
  waiting for transfers between devices  15.6 us (16%)
  starting transfers between devices  9.42 us (10%)
  local copies, waits for them, and re-layouts  2.68 us (3%)
    pallas_call x1, Pallas kernels, near_field(): pl.pallas_call(near_field_kernel, out_shape=(jax.ShapeDtypeStruct((slices...  23 us
    all_to_all x1, blocking collectives, on_device(): lax.all_to_all(rounded, 'sk', split_axis=0, concat_axis=0, tiled=True)  16.9 us
    all_to_all x1, blocking collectives, on_device(): lax.all_to_all(slab, ('child', 'sk'), split_axis=0, concat_axis=0, tiled=...  13.2 us
    pallas_call x1, Pallas kernels, cholesky(): pl.pallas_call(cholesky_kernel, out_shape=(jax.ShapeDtypeStruct((wide, 2...  11 us
    all_to_all x1, waiting for transfers between devices, on_device(): lax.all_to_all(sums, ('child', 'sk'), split_axis=0, concat_axis=0, tiled=...  10.9 us
    ppermute x1, waiting for transfers between devices, on_device(): lax.ppermute(edge(positions[:, :margin], sketch[:, :margin]), clus, backw...  4.47 us
    all_to_all x1, starting transfers between devices, on_device(): lax.all_to_all(sums, ('child', 'sk'), split_axis=0, concat_axis=0, tiled=...  3.82 us
    ppermute x1, starting transfers between devices, on_device(): lax.ppermute(edge(positions[:, -margin:], sketch[:, -margin:]), clus, for...  3.68 us
  transfers between devices with their start and end apart: 3, of which 3 were waited for; matrix products, arithmetic and copies ran while one was open for 0% of the time, Pallas kernels for 0%

profile of v1, /device:TPU:161, one launch (start us, length us, event | category | flops | bytes accessed | tf_op | source)
XLA Modules:
  0.0 95.7 jit_solution(10258610321039850403)
XLA Ops:
  0.6 0.0 copy-start
  0.6 0.8 fusion.8
  1.6 1.0 %fusion.12 = (bf16[64,1024]{1,0:T(8,128)(2,1)S(1)}, bf16[64,1024]{1,0:T(8,128)(2,1)S(1)}) fusion(bf16[64,8192]{1,0:T(8,128)(2,1)} %sk.1), kind=kLoop, calls=%fused_computation.23 | loop fusion | bytes 524288 | tf_op jit(solution)/shard_map/slice | solution.py:329
  2.6 3.7 %collective-permute-start = (bf16[80,1024]{1,0:T(8,128)(2,1)S(1)}, bf16[80,1024]{1,0:T(8,128)(2,1)S(1)}, u32[]{:S(2)}, u32[]{:S(2)}) collective-permute-start(bf16[80,1024]{1,0:T(8,128)(2,1)S(1)} %fusion.2), channel_id=1, source_target_pairs={{0,4},{4,8},{8,12},{12,16},{16,20},{20,24},{24,28},{28,32},{32,36}... | collective-permute-start | bytes 491528 | tf_op jit(solution)/shard_map/ppermute | solution.py:328
  6.4 1.9 %collective-permute-start.1 = (bf16[80,1024]{1,0:T(8,128)(2,1)S(1)}, bf16[80,1024]{1,0:T(8,128)(2,1)S(1)}, u32[]{:S(2)}, u32[]{:S(2)}) collective-permute-start(bf16[80,1024]{1,0:T(8,128)(2,1)S(1)} %fusion.3), channel_id=1, source_target_pairs={{4,0},{8,4},{12,8},{16,12},{20,16},{24,20},{28,24},{32,28},{36,32}... | collective-permute-start | bytes 491528 | tf_op jit(solution)/shard_map/ppermute | solution.py:329
  8.3 0.2 collective-permute-done.low
  8.5 4.5 %collective-permute-done.1.high = bf16[80,1024]{1,0:T(8,128)(2,1)S(1)} collective-permute-done((bf16[80,1024]{1,0:T(8,128)(2,1)S(1)}, bf16[80,1024]{1,0:T(8,128)(2,1)S(1)}, u32[]{:S(2)}, u32[]{:S(2)}) %collective-permute-start.1) | collective-permute-done | bytes 163872 | tf_op jit(solution)/shard_map/ppermute | solution.py:329
  13.0 0.0 copy-done
  13.0 0.0 copy-start.1
  13.0 0.9 copy-done.1
  13.9 0.0 copy-start.2
  13.9 0.7 copy-done.2
  14.6 23.0 %near_field.1 = (f32[64,8192]{1,0:T(8,128)}, bf16[4,64,2048]{2,1,0:T(8,128)(2,1)S(1)}) custom-call(f32[3,8192]{1,0:T(4,128)S(1)} %copy-done.1, bf16[64,8192]{1,0:T(8,128)(2,1)S(1)} %copy-done, bf16[80,1024]{1,0:T(8,128)(2,1)S(1)} %collective-permute-done.low, bf16[80,1024]{1,0:T(8,128)(2,1)S(1)} %collective-permute-done.1.high, s32[9,32]{1,0:T(8,128)S(1)} %bitcast.22), custom_call_target="tpu_custom_call" | custom-call | tf_op jit(solution)/shard_map/near_field/pallas_call | solution.py:147
  37.7 16.9 %all_to_all.15.points = bf16[4,64,2048]{2,1,0:T(8,128)(2,1)S(1)} all-to-all(bf16[4,64,2048]{2,1,0:T(8,128)(2,1)S(1)} %get-tuple-element.10), channel_id=1, replica_groups=mesh['tree'=32,'child'=4,'sk'=4] {'sk'}, dimensions={0} | all-to-all | bytes 2097152 | tf_op jit(solution)/shard_map/all_to_all | solution.py:331
  54.5 0.5 partial_gram.1
  55.0 13.2 %all_to_all.16.parts = f32[16,24,128]{2,1,0:T(8,128)} all-to-all(f32[16,24,128]{2,1,0:T(8,128)S(1)} %bitcast.21), channel_id=1, replica_groups=mesh['tree'=32,'child'=4,'sk'=4] {'child','sk'}, dimensions={0} | all-to-all | bytes 393216 | tf_op jit(solution)/shard_map/all_to_all | solution.py:335
  68.2 1.8 %combine.1 = f32[4,4,3,24,128]{4,3,2,1,0:T(8,128)} custom-call(f32[16,24,128]{2,1,0:T(8,128)} %all_to_all.16.parts), custom_call_target="tpu_custom_call" | custom-call | tf_op jit(solution)/shard_map/combine/pallas_call | solution.py:205
  70.0 3.8 %all-to-all-start.2 = ((f32[16,72,128]{2,1,0:T(8,128)}), f32[16,72,128]{2,1,0:T(8,128)S(1)}, u32[]{:S(2)}, u32[]{:S(2)}) async-start(f32[16,72,128]{2,1,0:T(8,128)} %bitcast.23), calls=%async_computation.2 | async-start | bytes 1179648 | tf_op jit(solution)/shard_map/all_to_all | solution.py:338
  73.8 10.9 %all-to-all-done.2 = f32[16,72,128]{2,1,0:T(8,128)S(1)} async-done(((f32[16,72,128]{2,1,0:T(8,128)}), f32[16,72,128]{2,1,0:T(8,128)S(1)}, u32[]{:S(2)}, u32[]{:S(2)}) %all-to-all-start.2) | async-done | bytes 589856 | tf_op jit(solution)/shard_map/all_to_all | solution.py:338
  84.7 11.0 %cholesky.1 = (f32[64,256]{1,0:T(8,128)}, f32[64,256]{1,0:T(8,128)}, f32[64,256]{1,0:T(8,128)}) custom-call(s32[1]{0:T(128)} %bitcast.7.place, f32[16,3,24,128]{3,2,1,0:T(8,128)S(1)} %bitcast.20), custom_call_target="tpu_custom_call" | custom-call | tf_op jit(solution)/shard_map/cholesky/pallas_call | solution.py:301
  (7 shorter events, 0.2 us)
Async XLA Ops:
  0.6 12.4 %copy-start = (bf16[64,8192]{1,0:T(8,128)(2,1)S(1)}, bf16[64,8192]{1,0:T(8,128)(2,1)}, u32[]{:S(2)}) copy-start(bf16[64,8192]{1,0:T(8,128)(2,1)} %sk.1) | copy-start | bytes 3145732
  2.6 5.9 %collective-permute-start = (bf16[80,1024]{1,0:T(8,128)(2,1)S(1)}, bf16[80,1024]{1,0:T(8,128)(2,1)S(1)}, u32[]{:S(2)}, u32[]{:S(2)}) collective-permute-start(bf16[80,1024]{1,0:T(8,128)(2,1)S(1)} %fusion.2), channel_id=1, source_target_pairs={{0,4},{4,8},{8,12},{12,16},{16,20},{20,24},{24,28},{28,32},{32,36}... | collective-permute-start | bytes 491528 | tf_op jit(solution)/shard_map/ppermute | solution.py:328
  6.4 6.6 %collective-permute-start.1 = (bf16[80,1024]{1,0:T(8,128)(2,1)S(1)}, bf16[80,1024]{1,0:T(8,128)(2,1)S(1)}, u32[]{:S(2)}, u32[]{:S(2)}) collective-permute-start(bf16[80,1024]{1,0:T(8,128)(2,1)S(1)} %fusion.3), channel_id=1, source_target_pairs={{4,0},{8,4},{12,8},{16,12},{20,16},{24,20},{28,24},{32,28},{36,32}... | collective-permute-start | bytes 491528 | tf_op jit(solution)/shard_map/ppermute | solution.py:329
  13.0 0.9 copy-start.1
  13.9 0.7 copy-start.2
  70.0 14.7 %all-to-all-start.2 = ((f32[16,72,128]{2,1,0:T(8,128)}), f32[16,72,128]{2,1,0:T(8,128)S(1)}, u32[]{:S(2)}, u32[]{:S(2)}) async-start(f32[16,72,128]{2,1,0:T(8,128)} %bitcast.23), calls=%async_computation.2 | async-start | bytes 1179648 | tf_op jit(solution)/shard_map/all_to_all | solution.py:338

commit v2 on v1

--- a/solution.py
+++ b/solution.py
@@ -1,3 +1,4 @@
+import functools
 import math
 
 import jax
@@ -19,10 +20,16 @@
 SHIFT = 64
 
 
-def near_field_kernel(pos, sk, low, high, near, image, rounded, across, along, cols, acc, held, todo):
+def near_field_kernel(
+    pos_far, sk, low, high, near_far, image, rounded, pos, near, across, along, cols, acc, held, todo, arrived
+):
     slices, rows = sk.shape
     own = rows // CS
     half = CS // 2
+    fetch_pos = pltpu.make_async_copy(pos_far, pos, arrived.at[0])
+    fetch_near = pltpu.make_async_copy(near_far, near, arrived.at[1])
+    fetch_pos.start()
+    fetch_near.start()
     last = own + 2 * H
 
     def joined(block):
@@ -36,16 +43,19 @@
     for slot in range(last):
         if slot < H:
             a = slot * CS
-            block, p = low[:slices, a : a + CS], joined(low[:, a : a + CS])
+            block = low[:slices, a : a + CS]
+            across[slot] = joined(low[:, a : a + CS])
         elif slot < H + own:
-            a = (slot - H) * CS
-            block, p = sk[:, a : a + CS], pos[:, a : a + CS]
+            block = sk[:, (slot - H) * CS : (slot - H + 1) * CS]
         else:
             a = (slot - H - own) * CS
-            block, p = high[:slices, a : a + CS], joined(high[:, a : a + CS])
+            block = high[:slices, a : a + CS]
+            across[slot] = joined(high[:, a : a + CS])
         cols[slot] = block
-        across[slot] = p
         acc[slot] = jnp.zeros((slices, CS), jnp.float32)
+    fetch_pos.wait()
+    for c in range(own):
+        across[c + H] = pos[:, c * CS : (c + 1) * CS]
     cols[last] = jnp.zeros((slices, CS), jnp.bfloat16)
     along[last] = jnp.zeros((CS, 384), jnp.float32)
     across[last] = jnp.zeros((3, CS), jnp.float32)
@@ -71,6 +81,7 @@
     def product_t(x, t):
         return lax.dot_general(x, t, (((1,), (1,)), ((), ())), preferred_element_type=jnp.float32)
 
+    fetch_near.wait()
     count = jnp.int32(UNROLL)
     for s in range(H):
         for d in range(s + 1, H + 1):
@@ -144,21 +155,25 @@
     slices, rows = sk.shape
     slots = rows // CS + 2 * H + 1
     whole = pl.BlockSpec(memory_space=pltpu.VMEM)
+    far = pl.BlockSpec(memory_space=pltpu.HBM)
     return pl.pallas_call(
         near_field_kernel,
         out_shape=(
             jax.ShapeDtypeStruct((slices, rows), jnp.float32),
             jax.ShapeDtypeStruct((shares, slices, rows // shares), jnp.bfloat16),
         ),
-        in_specs=[whole, whole, whole, whole, pl.BlockSpec(memory_space=pltpu.SMEM)],
+        in_specs=[far, whole, whole, whole, far],
         out_specs=(whole, whole),
         scratch_shapes=[
+            pltpu.VMEM(pos.shape, jnp.float32),
+            pltpu.SMEM(near.shape, jnp.int32),
             pltpu.VMEM((slots, 3, CS), jnp.float32),
             pltpu.VMEM((slots, CS, 3 * 128), jnp.float32),
             pltpu.VMEM((slots, slices, CS), jnp.bfloat16),
             pltpu.VMEM((slots, slices, CS), jnp.float32),
             pltpu.VMEM((UNROLL, CS, CS), jnp.bfloat16),
             pltpu.SMEM((slots * H + 4 * UNROLL,), jnp.int32),
+            pltpu.SemaphoreType.DMA((2,)),
         ],
         compiler_params=pltpu.CompilerParams(vmem_limit_bytes=36 * MIB),
         name="near_field",
@@ -168,45 +183,27 @@
 def gram_kernel(points, out, *, scale):
     whole = points[...].reshape(-1, points.shape[-1])
     half = whole.shape[0] // 2
+    part = half // 2
     product = lax.dot_general(whole, whole, (((1,), (1,)), ((), ())), preferred_element_type=jnp.float32) * scale
-    out[:half] = product[:half, :half]
-    out[half : 2 * half] = product[:half, half:]
-    out[2 * half :] = product[half:, half:]
-
-
-def partial_gram(points, scale):
+    lane = lax.broadcasted_iota(jnp.int32, (part, half), 1)
+    corner = pltpu.roll(product[half + part :, half:], part, 1)
+    mixed = jnp.where(lane < part, corner, product[part:half, :half])
+    for i in range(out.shape[0]):
+        out[i, :part] = product[:part, :half]
+        out[i, part : 2 * part] = product[:part, half:]
+        out[i, 2 * part : 3 * part] = product[part:half, half:]
+        out[i, 3 * part : 4 * part] = product[half : half + part, half:]
+        out[i, 4 * part :] = mixed
+
+
+def partial_gram(points, scale, copies):
     half = points.shape[0] * points.shape[1] // 2
     return pl.pallas_call(
         lambda points, out: gram_kernel(points, out, scale=scale),
-        out_shape=jax.ShapeDtypeStruct((3 * half, half), jnp.float32),
+        out_shape=jax.ShapeDtypeStruct((copies, 5 * half // 2, half), jnp.float32),
         compiler_params=pltpu.CompilerParams(vmem_limit_bytes=32 * MIB),
         name="partial_gram",
     )(points)
-
-
-def combine_kernel(parts, out):
-    k, s = out.shape[0], out.shape[1]
-    nodes = []
-    for i in range(k):
-        total = parts[i * s]
-        for j in range(1, s):
-            total = total + parts[i * s + j]
-        nodes.append(total)
-    pairs = [(nodes[i] + nodes[i + 1]) * 0.5 for i in range(0, k, 2)]
-    group = (pairs[0] + pairs[1]) * 0.5
-    for i in range(k):
-        for j in range(s):
-            out[i, j, 0] = nodes[i]
-            out[i, j, 1] = pairs[i // 2]
-            out[i, j, 2] = group
-
-
-def combine(parts, k, s):
-    return pl.pallas_call(
-        combine_kernel,
-        out_shape=jax.ShapeDtypeStruct((k, s, 3) + parts.shape[1:], jnp.float32),
-        name="combine",
-    )(parts)
 
 
 def pieces(value):
@@ -217,19 +214,30 @@
     return high, mid, low
 
 
-def cholesky_kernel(place, slabs, first, second, third, work, upper):
-    sources, mats, depth, half = slabs.shape
+def cholesky_kernel(place, *refs, mats, averages):
+    grams, outs, (work, upper) = refs[: -mats - 2], refs[-mats - 2 : -2], refs[-2:]
+    half = work.shape[1] // 2
+    part = half // 2
     n = 2 * half
-    for j in range(sources):
-        for t in range(0, depth, 8):
-            row = j * depth + t
-            block, at = row // half, row % half
-            for m in range(mats):
-                value = slabs[j, m, t : t + 8]
-                if block < 2:
-                    work[m, at : at + 8, block * half : (block + 1) * half] = value
-                else:
-                    work[m, half + at : half + at + 8, half:] = value
+    for m in range(mats):
+        for block in range(5):
+            rows = slice(block * part, (block + 1) * part)
+            value = grams[0][rows]
+            if averages:
+                value = (value + grams[1][rows]) * 0.5
+                if m == 1:
+                    value = (value + (grams[2][rows] + grams[3][rows]) * 0.5) * 0.5
+            if block == 0:
+                work[m, :part, :half] = value
+            elif block == 1:
+                work[m, :part, half:] = value
+            elif block == 2:
+                work[m, part:half, half:] = value
+            elif block == 3:
+                work[m, half : half + part, half:] = value
+            else:
+                work[m, part:half, :half] = value
+                work[m, half + part :, half:] = pltpu.roll(value, part, 1)
     for m in range(mats):
         upper[m, half:, :half] = jnp.zeros((half, half), jnp.float32)
     rowid = lax.broadcasted_iota(jnp.int32, (8, 128), 0)
@@ -266,6 +274,7 @@
                     row = spread(rows[m][hq][w][r : r + 1, :])
                     for h in range(hq, 2):
                         rows[m][h][w] = rows[m][h][w] - factor[h] * row
+        start = j0 + PANEL
         for m in range(mats):
             done = jnp.concatenate(
                 [
@@ -275,38 +284,40 @@
                 axis=0,
             )
             upper[m, j0 : j0 + PANEL, lane0:] = done
-            start = j0 + PANEL
             if start < n:
                 high, mid, low = pieces(done)
+                left = jnp.concatenate([high, high, mid, high, mid, low], axis=0)
+                right = jnp.concatenate([high, mid, high, low, mid, high], axis=0)
                 skip = (0 if start < half else half) - lane0
-                left = jnp.concatenate([high, high, mid, high, mid, low], axis=0)[:, skip:]
-                right = jnp.concatenate([high, mid, high, low, mid, high], axis=0)[:, skip:]
-                product = lax.dot_general(left, right, (((0,), (0,)), ((), ())), preferred_element_type=jnp.float32)
+                product = lax.dot_general(
+                    left[:, skip:], right[:, skip:], (((0,), (0,)), ((), ())), preferred_element_type=jnp.float32
+                )
                 if start < half:
                     work[m, start:half, :] = work[m, start:half, :] - product[start:half, :]
                     work[m, half:, half:] = work[m, half:, half:] - product[half:, half:]
                 else:
                     work[m, start:, half:] = work[m, start:, half:] - product[start - half :, :]
-    wide = first.shape[0]
+    wide = outs[0].shape[0]
     begin = pl.multiple_of(place[0] * wide, wide)
     i = lax.broadcasted_iota(jnp.int32, (wide, n), 0) + begin
     j = lax.broadcasted_iota(jnp.int32, (wide, n), 1)
-    for m, out in enumerate((first, second, third)):
+    for m, out in enumerate(outs):
         out[...] = jnp.where(j >= i, upper[m, pl.ds(begin, wide), :], 0.0)
 
 
-def cholesky(place, slabs, wide):
-    half = slabs.shape[3]
+def cholesky(place, grams, wide, mats, name):
+    half = grams[0].shape[1]
     whole = pl.BlockSpec(memory_space=pltpu.VMEM)
+    kernel = functools.partial(cholesky_kernel, mats=mats, averages=len(grams) > 1)
     return pl.pallas_call(
-        cholesky_kernel,
-        out_shape=(jax.ShapeDtypeStruct((wide, 2 * half), jnp.float32),) * 3,
-        in_specs=[pl.BlockSpec(memory_space=pltpu.SMEM), whole],
-        out_specs=(whole,) * 3,
-        scratch_shapes=[pltpu.VMEM((3, 2 * half, 2 * half), jnp.float32)] * 2,
+        kernel,
+        out_shape=(jax.ShapeDtypeStruct((wide, 2 * half), jnp.float32),) * mats,
+        in_specs=[pl.BlockSpec(memory_space=pltpu.SMEM)] + [whole] * len(grams),
+        out_specs=(whole,) * mats,
+        scratch_shapes=[pltpu.VMEM((mats, 2 * half, 2 * half), jnp.float32)] * 2,
         compiler_params=pltpu.CompilerParams(vmem_limit_bytes=32 * MIB),
-        name="cholesky",
-    )(place, slabs)
+        name=name,
+    )(place, *grams)
 
 
 def edge(positions, sketch):
@@ -329,16 +340,14 @@
     high = lax.ppermute(edge(positions[:, :margin], sketch[:, :margin]), clus, backward)
     image, rounded = near_field(positions, sketch, low, high, near.T, shares)
     traded = lax.all_to_all(rounded, "sk", split_axis=0, concat_axis=0, tiled=True)
-    gram = partial_gram(traded, 1.0 / rows)
-    family = FAMILY * shares
-    slab = gram.reshape(family, -1, gram.shape[1])
-    parts = lax.all_to_all(slab, ("child", "sk"), split_axis=0, concat_axis=0, tiled=True)
-    sums = combine(parts, FAMILY, shares)
-    sums = sums.reshape(family, 3 * slab.shape[1], slab.shape[2])
-    slabs = lax.all_to_all(sums, ("child", "sk"), split_axis=0, concat_axis=0, tiled=True)
-    slabs = slabs.reshape(family, 3, slab.shape[1], slab.shape[2])
+    shared = partial_gram(traded, 1.0 / rows, shares)
+    parts = lax.all_to_all(shared, "sk", split_axis=0, concat_axis=0, tiled=True)
+    node = jnp.sum(parts, axis=0)
+    siblings = [lax.ppermute(node, "child", [(i, i ^ d) for i in range(FAMILY)]) for d in range(1, FAMILY)]
     place = lax.axis_index("sk").astype(jnp.int32).reshape(1)
-    return (image, *(factor.T for factor in cholesky(place, slabs, slices)))
+    first = cholesky(place, [node], slices, 1, "node_factor")
+    others = cholesky(place, [node, *siblings], slices, 2, "upper_factors")
+    return (image, *(factor.T for factor in (*first, *others)))
 
 
 def solution(mesh):

time: 96.1 us -> 99.1 us (1.031)
  the two profiles are of different devices: /device:TPU:161 before, /device:TPU:455 now
where the time goes in v2:
time: 99.1 us; the launch traced here: 98.7 us
  Pallas kernels  41.7 us (42%)
  blocking collectives  32 us (32%)
  starting transfers between devices  13.7 us (14%)
  waiting for transfers between devices  6.83 us (7%)
  local copies, waits for them, and re-layouts  2.68 us (3%)
    pallas_call x1, Pallas kernels, near_field(): pl.pallas_call(near_field_kernel, out_shape=(jax.ShapeDtypeStruct((slices...  23.4 us
    all_to_all x1, blocking collectives, on_device(): lax.all_to_all(rounded, 'sk', split_axis=0, concat_axis=0, tiled=True)  18.9 us
    pallas_call x2, Pallas kernels, cholesky(): pl.pallas_call(kernel, out_shape=(jax.ShapeDtypeStruct((wide, 2 * half),...  17.8 us
    all_to_all x1, blocking collectives, on_device(): lax.all_to_all(shared, 'sk', split_axis=0, concat_axis=0, tiled=True)  13.1 us
    ppermute x3, starting transfers between devices, on_device(): lax.ppermute(node, 'child', [(i, i ^ d) for i in range(FAMILY)])  8.66 us
    ppermute x1, waiting for transfers between devices, on_device(): lax.ppermute(edge(positions[:, :margin], sketch[:, :margin]), clus, backw...  6.58 us
    ppermute x1, starting transfers between devices, on_device(): lax.ppermute(edge(positions[:, -margin:], sketch[:, -margin:]), clus, for...  3.12 us
  transfers between devices with their start and end apart: 5, of which 2 were waited for; matrix products, arithmetic and copies ran while one was open for 0% of the time, Pallas kernels for 8%

profile of v2, /device:TPU:455, one launch (start us, length us, event | category | flops | bytes accessed | tf_op | source)
XLA Modules:
  0.0 98.7 jit_solution(8881569848229731741)
XLA Ops:
  0.6 0.0 copy-start
  0.6 0.8 fusion.8
  1.6 1.0 %fusion.12 = (bf16[64,1024]{1,0:T(8,128)(2,1)S(1)}, bf16[64,1024]{1,0:T(8,128)(2,1)S(1)}) fusion(bf16[64,8192]{1,0:T(8,128)(2,1)} %sk.1), kind=kLoop, calls=%fused_computation.23 | loop fusion | bytes 524288 | tf_op jit(solution)/shard_map/slice | solution.py:340
  2.6 3.1 %collective-permute-start = (bf16[80,1024]{1,0:T(8,128)(2,1)S(1)}, bf16[80,1024]{1,0:T(8,128)(2,1)S(1)}, u32[]{:S(2)}, u32[]{:S(2)}) collective-permute-start(bf16[80,1024]{1,0:T(8,128)(2,1)S(1)} %fusion.2), channel_id=1, source_target_pairs={{0,4},{4,8},{8,12},{12,16},{16,20},{20,24},{24,28},{28,32},{32,36}... | collective-permute-start | bytes 491528 | tf_op jit(solution)/shard_map/ppermute | solution.py:339
  5.8 1.9 %collective-permute-start.1 = (bf16[80,1024]{1,0:T(8,128)(2,1)S(1)}, bf16[80,1024]{1,0:T(8,128)(2,1)S(1)}, u32[]{:S(2)}, u32[]{:S(2)}) collective-permute-start(bf16[80,1024]{1,0:T(8,128)(2,1)S(1)} %fusion.3), channel_id=1, source_target_pairs={{4,0},{8,4},{12,8},{16,12},{20,16},{24,20},{28,24},{32,28},{36,32}... | collective-permute-start | bytes 491528 | tf_op jit(solution)/shard_map/ppermute | solution.py:340
  7.7 0.2 collective-permute-done.low
  8.0 6.6 %collective-permute-done.1.high = bf16[80,1024]{1,0:T(8,128)(2,1)S(1)} collective-permute-done((bf16[80,1024]{1,0:T(8,128)(2,1)S(1)}, bf16[80,1024]{1,0:T(8,128)(2,1)S(1)}, u32[]{:S(2)}, u32[]{:S(2)}) %collective-permute-start.1) | collective-permute-done | bytes 163872 | tf_op jit(solution)/shard_map/ppermute | solution.py:340
  14.6 0.0 copy-done
  14.6 0.0 copy-start.1
  14.6 0.9 copy-done.1
  15.5 0.0 copy-start.2
  15.5 0.7 copy-done.2
  16.2 23.4 %near_field.1 = (f32[64,8192]{1,0:T(8,128)}, bf16[4,64,2048]{2,1,0:T(8,128)(2,1)S(1)}) custom-call(f32[3,8192]{1,0:T(4,128)S(1)} %copy-done.1, bf16[64,8192]{1,0:T(8,128)(2,1)S(1)} %copy-done, bf16[80,1024]{1,0:T(8,128)(2,1)S(1)} %collective-permute-done.low, bf16[80,1024]{1,0:T(8,128)(2,1)S(1)} %collective-permute-done.1.high, s32[9,32]{1,0:T(8,128)S(1)} %bitcast.17), custom_call_target="tpu_custom_call" | custom-call | tf_op jit(solution)/shard_map/near_field/pallas_call | solution.py:159
  39.6 18.9 %all_to_all.10.points = bf16[4,64,2048]{2,1,0:T(8,128)(2,1)S(1)} all-to-all(bf16[4,64,2048]{2,1,0:T(8,128)(2,1)S(1)} %get-tuple-element.9), channel_id=1, replica_groups=mesh['tree'=32,'child'=4,'sk'=4] {'sk'}, dimensions={0} | all-to-all | bytes 2097152 | tf_op jit(solution)/shard_map/all_to_all | solution.py:342
  58.5 0.5 partial_gram.1
  59.0 13.1 %all_to_all.11 = f32[4,320,128]{2,1,0:T(8,128)S(1)} all-to-all(f32[4,320,128]{2,1,0:T(8,128)S(1)} %partial_gram.1), channel_id=1, replica_groups=mesh['tree'=32,'child'=4,'sk'=4] {'sk'}, dimensions={0} | all-to-all | bytes 1310720 | tf_op jit(solution)/shard_map/all_to_all | solution.py:344
  72.2 3.0 %collective-permute-start.2 = (f32[320,128]{1,0:T(8,128)S(1)}, f32[320,128]{1,0:T(8,128)S(1)}, u32[]{:S(2)}, u32[]{:S(2)}) collective-permute-start(f32[320,128]{1,0:T(8,128)S(1)} %reduce_sum.9.refs_0_), channel_id=1, source_target_pairs={{0,4},{4,0},{8,12},{12,8},{1,5},{5,1},{9,13},{13,9},{2,6},{6,2},{1... | collective-permute-start | bytes 491528 | tf_op jit(solution)/shard_map/ppermute | solution.py:346
  75.2 1.9 %collective-permute-start.3 = (f32[320,128]{1,0:T(8,128)S(1)}, f32[320,128]{1,0:T(8,128)S(1)}, u32[]{:S(2)}, u32[]{:S(2)}) collective-permute-start(f32[320,128]{1,0:T(8,128)S(1)} %reduce_sum.9.refs_0_), channel_id=1, source_target_pairs={{0,8},{4,12},{8,0},{12,4},{1,9},{5,13},{9,1},{13,5},{2,10},{6,14},... | collective-permute-start | bytes 491528 | tf_op jit(solution)/shard_map/ppermute | solution.py:346
  77.2 3.7 %collective-permute-start.4 = (f32[320,128]{1,0:T(8,128)S(1)}, f32[320,128]{1,0:T(8,128)S(1)}, u32[]{:S(2)}, u32[]{:S(2)}) collective-permute-start(f32[320,128]{1,0:T(8,128)S(1)} %reduce_sum.9.refs_0_), channel_id=1, source_target_pairs={{0,12},{4,8},{8,4},{12,0},{1,13},{5,9},{9,5},{13,1},{2,14},{6,10},... | collective-permute-start | bytes 491528 | tf_op jit(solution)/shard_map/ppermute | solution.py:346
  80.9 8.1 %node_factor.1 = f32[64,256]{1,0:T(8,128)} custom-call(s32[1]{0:T(128)} %bitcast.7.place, f32[320,128]{1,0:T(8,128)S(1)} %reduce_sum.9.refs_0_), custom_call_target="tpu_custom_call" | custom-call | tf_op jit(solution)/shard_map/node_factor/pallas_call | solution.py:312
  89.0 0.0 collective-permute-done.2.refs_1_
  89.0 0.0 collective-permute-done.3.refs_2_
  89.0 0.0 collective-permute-done.4.refs_3_
  89.0 9.6 %upper_factors.1 = (f32[64,256]{1,0:T(8,128)}, f32[64,256]{1,0:T(8,128)}) custom-call(s32[1]{0:T(128)} %bitcast.7.place, f32[320,128]{1,0:T(8,128)S(1)} %reduce_sum.9.refs_0_, f32[320,128]{1,0:T(8,128)S(1)} %collective-permute-done.2.refs_1_, f32[320,128]{1,0:T(8,128)S(1)} %collective-permute-done.3.refs_2_, f32[320,128]{1,0:T(8,128)S(1)} %collective-permute-done.4.refs_3_), custom_call_target="tpu_custom_call" | custom-call | tf_op jit(solution)/shard_map/upper_factors/pallas_call | solution.py:312
  (8 shorter events, 0.2 us)
Async XLA Ops:
  0.6 13.9 %copy-start = (bf16[64,8192]{1,0:T(8,128)(2,1)S(1)}, bf16[64,8192]{1,0:T(8,128)(2,1)}, u32[]{:S(2)}) copy-start(bf16[64,8192]{1,0:T(8,128)(2,1)} %sk.1) | copy-start | bytes 3145732
  2.6 5.4 %collective-permute-start = (bf16[80,1024]{1,0:T(8,128)(2,1)S(1)}, bf16[80,1024]{1,0:T(8,128)(2,1)S(1)}, u32[]{:S(2)}, u32[]{:S(2)}) collective-permute-start(bf16[80,1024]{1,0:T(8,128)(2,1)S(1)} %fusion.2), channel_id=1, source_target_pairs={{0,4},{4,8},{8,12},{12,16},{16,20},{20,24},{24,28},{28,32},{32,36}... | collective-permute-start | bytes 491528 | tf_op jit(solution)/shard_map/ppermute | solution.py:339
  5.8 8.7 %collective-permute-start.1 = (bf16[80,1024]{1,0:T(8,128)(2,1)S(1)}, bf16[80,1024]{1,0:T(8,128)(2,1)S(1)}, u32[]{:S(2)}, u32[]{:S(2)}) collective-permute-start(bf16[80,1024]{1,0:T(8,128)(2,1)S(1)} %fusion.3), channel_id=1, source_target_pairs={{4,0},{8,4},{12,8},{16,12},{20,16},{24,20},{28,24},{32,28},{36,32}... | collective-permute-start | bytes 491528 | tf_op jit(solution)/shard_map/ppermute | solution.py:340
  14.6 0.9 copy-start.1
  15.5 0.7 copy-start.2
  72.2 16.8 %collective-permute-start.2 = (f32[320,128]{1,0:T(8,128)S(1)}, f32[320,128]{1,0:T(8,128)S(1)}, u32[]{:S(2)}, u32[]{:S(2)}) collective-permute-start(f32[320,128]{1,0:T(8,128)S(1)} %reduce_sum.9.refs_0_), channel_id=1, source_target_pairs={{0,4},{4,0},{8,12},{12,8},{1,5},{5,1},{9,13},{13,9},{2,6},{6,2},{1... | collective-permute-start | bytes 491528 | tf_op jit(solution)/shard_map/ppermute | solution.py:346
  75.2 13.8 %collective-permute-start.3 = (f32[320,128]{1,0:T(8,128)S(1)}, f32[320,128]{1,0:T(8,128)S(1)}, u32[]{:S(2)}, u32[]{:S(2)}) collective-permute-start(f32[320,128]{1,0:T(8,128)S(1)} %reduce_sum.9.refs_0_), channel_id=1, source_target_pairs={{0,8},{4,12},{8,0},{12,4},{1,9},{5,13},{9,1},{13,5},{2,10},{6,14},... | collective-permute-start | bytes 491528 | tf_op jit(solution)/shard_map/ppermute | solution.py:346
  77.2 11.9 %collective-permute-start.4 = (f32[320,128]{1,0:T(8,128)S(1)}, f32[320,128]{1,0:T(8,128)S(1)}, u32[]{:S(2)}, u32[]{:S(2)}) collective-permute-start(f32[320,128]{1,0:T(8,128)S(1)} %reduce_sum.9.refs_0_), channel_id=1, source_target_pairs={{0,12},{4,8},{8,4},{12,0},{1,13},{5,9},{9,5},{13,1},{2,14},{6,10},... | collective-permute-start | bytes 491528 | tf_op jit(solution)/shard_map/ppermute | solution.py:346

commit v3 on v2

--- a/solution.py
+++ b/solution.py
@@ -1,4 +1,3 @@
-import functools
 import math
 
 import jax
@@ -21,14 +20,12 @@
 
 
 def near_field_kernel(
-    pos_far, sk, low, high, near_far, image, rounded, pos, near, across, along, cols, acc, held, todo, arrived
+    pos, sk, low, high, near_far, image, rounded, near, across, along, cols, acc, held, todo, arrived
 ):
     slices, rows = sk.shape
     own = rows // CS
     half = CS // 2
-    fetch_pos = pltpu.make_async_copy(pos_far, pos, arrived.at[0])
-    fetch_near = pltpu.make_async_copy(near_far, near, arrived.at[1])
-    fetch_pos.start()
+    fetch_near = pltpu.make_async_copy(near_far, near, arrived)
     fetch_near.start()
     last = own + 2 * H
 
@@ -53,9 +50,8 @@
             across[slot] = joined(high[:, a : a + CS])
         cols[slot] = block
         acc[slot] = jnp.zeros((slices, CS), jnp.float32)
-    fetch_pos.wait()
     for c in range(own):
-        across[c + H] = pos[:, c * CS : (c + 1) * CS]
+        across[c + H] = pos[c]
     cols[last] = jnp.zeros((slices, CS), jnp.bfloat16)
     along[last] = jnp.zeros((CS, 384), jnp.float32)
     across[last] = jnp.zeros((3, CS), jnp.float32)
@@ -86,7 +82,7 @@
     for s in range(H):
         for d in range(s + 1, H + 1):
             todo[count] = (s - d + H) * SHIFT + s + H
-            count = count + near[H - d, s]
+            count = count + near[s, H - d]
 
     def close_products(c, buf):
         x = cols[c]
@@ -110,7 +106,7 @@
         for u in range(2):
             for d in range(2, H + 1):
                 todo[count] = (c + u) * SHIFT + c + u + d
-                count = count + near[H + d, c + u - H]
+                count = count + near[c + u - H, H + d]
             copy_along(c + u + 3)
             close_tiles(c + u, 2 * u)
         return count
@@ -162,10 +158,9 @@
             jax.ShapeDtypeStruct((slices, rows), jnp.float32),
             jax.ShapeDtypeStruct((shares, slices, rows // shares), jnp.bfloat16),
         ),
-        in_specs=[far, whole, whole, whole, far],
+        in_specs=[whole, whole, whole, whole, far],
         out_specs=(whole, whole),
         scratch_shapes=[
-            pltpu.VMEM(pos.shape, jnp.float32),
             pltpu.SMEM(near.shape, jnp.int32),
             pltpu.VMEM((slots, 3, CS), jnp.float32),
             pltpu.VMEM((slots, CS, 3 * 128), jnp.float32),
@@ -173,7 +168,7 @@
             pltpu.VMEM((slots, slices, CS), jnp.float32),
             pltpu.VMEM((UNROLL, CS, CS), jnp.bfloat16),
             pltpu.SMEM((slots * H + 4 * UNROLL,), jnp.int32),
-            pltpu.SemaphoreType.DMA((2,)),
+            pltpu.SemaphoreType.DMA,
         ],
         compiler_params=pltpu.CompilerParams(vmem_limit_bytes=36 * MIB),
         name="near_field",
@@ -214,19 +209,15 @@
     return high, mid, low
 
 
-def cholesky_kernel(place, *refs, mats, averages):
-    grams, outs, (work, upper) = refs[: -mats - 2], refs[-mats - 2 : -2], refs[-2:]
+def cholesky_kernel(place, grams, *refs):
+    outs, (work, upper) = refs[:-2], refs[-2:]
+    mats = len(outs)
     half = work.shape[1] // 2
     part = half // 2
     n = 2 * half
     for m in range(mats):
         for block in range(5):
-            rows = slice(block * part, (block + 1) * part)
-            value = grams[0][rows]
-            if averages:
-                value = (value + grams[1][rows]) * 0.5
-                if m == 1:
-                    value = (value + (grams[2][rows] + grams[3][rows]) * 0.5) * 0.5
+            value = grams[m, block * part : (block + 1) * part]
             if block == 0:
                 work[m, :part, :half] = value
             elif block == 1:
@@ -305,19 +296,18 @@
         out[...] = jnp.where(j >= i, upper[m, pl.ds(begin, wide), :], 0.0)
 
 
-def cholesky(place, grams, wide, mats, name):
-    half = grams[0].shape[1]
+def cholesky(place, grams, wide):
+    mats, half = grams.shape[0], grams.shape[2]
     whole = pl.BlockSpec(memory_space=pltpu.VMEM)
-    kernel = functools.partial(cholesky_kernel, mats=mats, averages=len(grams) > 1)
     return pl.pallas_call(
-        kernel,
+        cholesky_kernel,
         out_shape=(jax.ShapeDtypeStruct((wide, 2 * half), jnp.float32),) * mats,
-        in_specs=[pl.BlockSpec(memory_space=pltpu.SMEM)] + [whole] * len(grams),
+        in_specs=[pl.BlockSpec(memory_space=pltpu.SMEM), whole],
         out_specs=(whole,) * mats,
         scratch_shapes=[pltpu.VMEM((mats, 2 * half, 2 * half), jnp.float32)] * 2,
         compiler_params=pltpu.CompilerParams(vmem_limit_bytes=32 * MIB),
-        name=name,
-    )(place, *grams)
+        name="cholesky",
+    )(place, grams)
 
 
 def edge(positions, sketch):
@@ -338,16 +328,18 @@
     backward = [(i + 1, i) for i in range(count - 1)]
     low = lax.ppermute(edge(positions[:, -margin:], sketch[:, -margin:]), clus, forward)
     high = lax.ppermute(edge(positions[:, :margin], sketch[:, :margin]), clus, backward)
-    image, rounded = near_field(positions, sketch, low, high, near.T, shares)
+    by_cluster = positions.reshape(3, -1, CS).transpose(1, 0, 2)
+    image, rounded = near_field(by_cluster, sketch, low, high, near, shares)
     traded = lax.all_to_all(rounded, "sk", split_axis=0, concat_axis=0, tiled=True)
     shared = partial_gram(traded, 1.0 / rows, shares)
     parts = lax.all_to_all(shared, "sk", split_axis=0, concat_axis=0, tiled=True)
     node = jnp.sum(parts, axis=0)
-    siblings = [lax.ppermute(node, "child", [(i, i ^ d) for i in range(FAMILY)]) for d in range(1, FAMILY)]
+    sibling = lambda value, d: lax.ppermute(value, "child", [(i, i ^ d) for i in range(FAMILY)])
+    pair = (node + sibling(node, 1)) * 0.5
+    group = (pair + sibling(pair, 2)) * 0.5
     place = lax.axis_index("sk").astype(jnp.int32).reshape(1)
-    first = cholesky(place, [node], slices, 1, "node_factor")
-    others = cholesky(place, [node, *siblings], slices, 2, "upper_factors")
-    return (image, *(factor.T for factor in (*first, *others)))
+    factors = cholesky(place, jnp.stack([node, pair, group]), slices)
+    return (image, *(factor.T for factor in factors))
 
 
 def solution(mesh):

time: 99.1 us -> 94 us (0.949)
  the two profiles are of different devices: /device:TPU:455 before, /device:TPU:288 now
where the time goes in v3:
time: 94 us; the launch traced here: 93.6 us
  blocking collectives  34.6 us (37%)
  Pallas kernels  33.3 us (35%)
  starting transfers between devices  11.7 us (12%)
  waiting for transfers between devices  9.43 us (10%)
  local copies, waits for them, and re-layouts  2.76 us (3%)
  other arithmetic  1.02 us (1%)
    pallas_call x1, Pallas kernels, near_field(): pl.pallas_call(near_field_kernel, out_shape=(jax.ShapeDtypeStruct((slices...  21.6 us
    all_to_all x1, blocking collectives, on_device(): lax.all_to_all(rounded, 'sk', split_axis=0, concat_axis=0, tiled=True)  20.8 us
    all_to_all x1, blocking collectives, on_device(): lax.all_to_all(shared, 'sk', split_axis=0, concat_axis=0, tiled=True)  13.8 us
    pallas_call x1, Pallas kernels, cholesky(): pl.pallas_call(cholesky_kernel, out_shape=(jax.ShapeDtypeStruct((wide, 2...  11.2 us
    ppermute x2, waiting for transfers between devices, on_device(): lax.ppermute(value, 'child', [(i, i ^ d) for i in range(FAMILY)])  7.39 us
    ppermute x1, starting transfers between devices, on_device(): lax.ppermute(edge(positions[:, :margin], sketch[:, :margin]), clus, backw...  5.75 us
    ppermute x2, starting transfers between devices, on_device(): lax.ppermute(value, 'child', [(i, i ^ d) for i in range(FAMILY)])  4.02 us
    ppermute x1, starting transfers between devices, on_device(): lax.ppermute(edge(positions[:, -margin:], sketch[:, -margin:]), clus, for...  1.92 us
  transfers between devices with their start and end apart: 4, of which 4 were waited for; matrix products, arithmetic and copies ran while one was open for 1% of the time, Pallas kernels for 0%

profile of v3, /device:TPU:288, one launch (start us, length us, event | category | flops | bytes accessed | tf_op | source)
XLA Modules:
  0.0 93.6 jit_solution(5430391143386266859)
XLA Ops:
  0.6 0.0 copy-start
  0.6 0.8 fusion.8
  1.6 1.0 %fusion.12 = (bf16[64,1024]{1,0:T(8,128)(2,1)S(1)}, bf16[64,1024]{1,0:T(8,128)(2,1)S(1)}) fusion(bf16[64,8192]{1,0:T(8,128)(2,1)} %sk.1), kind=kLoop, calls=%fused_computation.26 | loop fusion | bytes 524288 | tf_op jit(solution)/shard_map/slice | solution.py:330
  2.6 1.9 %collective-permute-start = (bf16[80,1024]{1,0:T(8,128)(2,1)S(1)}, bf16[80,1024]{1,0:T(8,128)(2,1)S(1)}, u32[]{:S(2)}, u32[]{:S(2)}) collective-permute-start(bf16[80,1024]{1,0:T(8,128)(2,1)S(1)} %fusion.2), channel_id=1, source_target_pairs={{0,4},{4,8},{8,12},{12,16},{16,20},{20,24},{24,28},{28,32},{32,36}... | collective-permute-start | bytes 491528 | tf_op jit(solution)/shard_map/ppermute | solution.py:329
  4.6 5.8 %collective-permute-start.1 = (bf16[80,1024]{1,0:T(8,128)(2,1)S(1)}, bf16[80,1024]{1,0:T(8,128)(2,1)S(1)}, u32[]{:S(2)}, u32[]{:S(2)}) collective-permute-start(bf16[80,1024]{1,0:T(8,128)(2,1)S(1)} %fusion.3), channel_id=1, source_target_pairs={{4,0},{8,4},{12,8},{16,12},{20,16},{24,20},{28,24},{32,28},{36,32}... | collective-permute-start | bytes 491528 | tf_op jit(solution)/shard_map/ppermute | solution.py:330
  10.4 0.8 copy.9.near_far
  11.2 0.2 collective-permute-done.low
  11.4 1.8 %collective-permute-done.1.high = bf16[80,1024]{1,0:T(8,128)(2,1)S(1)} collective-permute-done((bf16[80,1024]{1,0:T(8,128)(2,1)S(1)}, bf16[80,1024]{1,0:T(8,128)(2,1)S(1)}, u32[]{:S(2)}, u32[]{:S(2)}) %collective-permute-start.1) | collective-permute-done | bytes 163872 | tf_op jit(solution)/shard_map/ppermute | solution.py:330
  13.2 0.0 copy-done
  13.2 0.0 copy-start.1
  13.2 0.9 copy-done.1
  14.1 21.6 %near_field.1 = (f32[64,8192]{1,0:T(8,128)}, bf16[4,64,2048]{2,1,0:T(8,128)(2,1)S(1)}) custom-call(f32[32,3,256]{2,1,0:T(4,128)S(1)} %bitcast.23, bf16[64,8192]{1,0:T(8,128)(2,1)S(1)} %copy-done, bf16[80,1024]{1,0:T(8,128)(2,1)S(1)} %collective-permute-done.low, bf16[80,1024]{1,0:T(8,128)(2,1)S(1)} %collective-permute-done.1.high, s32[32,9]{1,0:T(8,128)S(1)} %copy.9.near_far), custom_call_target="tpu_custom_call" | custom-call | tf_op jit(solution)/shard_map/near_field/pallas_call | solution.py:155
  35.7 20.8 %all_to_all.10.points = bf16[4,64,2048]{2,1,0:T(8,128)(2,1)S(1)} all-to-all(bf16[4,64,2048]{2,1,0:T(8,128)(2,1)S(1)} %get-tuple-element.10), channel_id=1, replica_groups=mesh['tree'=32,'child'=4,'sk'=4] {'sk'}, dimensions={0} | all-to-all | bytes 2097152 | tf_op jit(solution)/shard_map/all_to_all | solution.py:333
  56.5 0.5 partial_gram.1
  57.0 13.8 %all_to_all.11 = f32[4,320,128]{2,1,0:T(8,128)S(1)} all-to-all(f32[4,320,128]{2,1,0:T(8,128)S(1)} %partial_gram.1), channel_id=1, replica_groups=mesh['tree'=32,'child'=4,'sk'=4] {'sk'}, dimensions={0} | all-to-all | bytes 1310720 | tf_op jit(solution)/shard_map/all_to_all | solution.py:335
  70.9 1.9 %collective-permute-start.2 = (f32[320,128]{1,0:T(8,128)S(1)}, f32[320,128]{1,0:T(8,128)S(1)}, u32[]{:S(2)}, u32[]{:S(2)}) collective-permute-start(f32[320,128]{1,0:T(8,128)S(1)} %reduce_sum.9), channel_id=1, source_target_pairs={{0,4},{4,0},{8,12},{12,8},{1,5},{5,1},{9,13},{13,9},{2,6},{6,2},{1... | collective-permute-start | bytes 491528 | tf_op jit(solution)/shard_map/ppermute | solution.py:337
  72.8 1.4 %collective-permute-done.2 = f32[320,128]{1,0:T(8,128)S(1)} collective-permute-done((f32[320,128]{1,0:T(8,128)S(1)}, f32[320,128]{1,0:T(8,128)S(1)}, u32[]{:S(2)}, u32[]{:S(2)}) %collective-permute-start.2) | collective-permute-done | bytes 163872 | tf_op jit(solution)/shard_map/ppermute | solution.py:337
  74.2 2.1 %collective-permute-start.3 = (f32[320,128]{1,0:T(8,128)S(1)}, f32[320,128]{1,0:T(8,128)S(1)}, u32[]{:S(2)}, u32[]{:S(2)}) collective-permute-start(f32[320,128]{1,0:T(8,128)S(1)} %add_multiply_fusion), channel_id=1, source_target_pairs={{0,8},{4,12},{8,0},{12,4},{1,9},{5,13},{9,1},{13,5},{2,10},{6,14},... | collective-permute-start | bytes 491528 | tf_op jit(solution)/shard_map/ppermute | solution.py:337
  76.3 6.0 %collective-permute-done.3 = f32[320,128]{1,0:T(8,128)S(1)} collective-permute-done((f32[320,128]{1,0:T(8,128)S(1)}, f32[320,128]{1,0:T(8,128)S(1)}, u32[]{:S(2)}, u32[]{:S(2)}) %collective-permute-start.3) | collective-permute-done | bytes 163872 | tf_op jit(solution)/shard_map/ppermute | solution.py:337
  82.4 11.2 %cholesky.1 = (f32[64,256]{1,0:T(8,128)}, f32[64,256]{1,0:T(8,128)}, f32[64,256]{1,0:T(8,128)}) custom-call(s32[1]{0:T(128)} %bitcast.8.place, f32[3,320,128]{2,1,0:T(8,128)S(1)} %pad_maximum_fusion.grams), custom_call_target="tpu_custom_call" | custom-call | tf_op jit(solution)/shard_map/cholesky/pallas_call | solution.py:302
  (11 shorter events, 0.3 us)
Async XLA Ops:
  0.6 12.6 %copy-start = (bf16[64,8192]{1,0:T(8,128)(2,1)S(1)}, bf16[64,8192]{1,0:T(8,128)(2,1)}, u32[]{:S(2)}) copy-start(bf16[64,8192]{1,0:T(8,128)(2,1)} %sk.1) | copy-start | bytes 3145732
  2.6 8.7 %collective-permute-start = (bf16[80,1024]{1,0:T(8,128)(2,1)S(1)}, bf16[80,1024]{1,0:T(8,128)(2,1)S(1)}, u32[]{:S(2)}, u32[]{:S(2)}) collective-permute-start(bf16[80,1024]{1,0:T(8,128)(2,1)S(1)} %fusion.2), channel_id=1, source_target_pairs={{0,4},{4,8},{8,12},{12,16},{16,20},{20,24},{24,28},{28,32},{32,36}... | collective-permute-start | bytes 491528 | tf_op jit(solution)/shard_map/ppermute | solution.py:329
  4.6 8.6 %collective-permute-start.1 = (bf16[80,1024]{1,0:T(8,128)(2,1)S(1)}, bf16[80,1024]{1,0:T(8,128)(2,1)S(1)}, u32[]{:S(2)}, u32[]{:S(2)}) collective-permute-start(bf16[80,1024]{1,0:T(8,128)(2,1)S(1)} %fusion.3), channel_id=1, source_target_pairs={{4,0},{8,4},{12,8},{16,12},{20,16},{24,20},{28,24},{32,28},{36,32}... | collective-permute-start | bytes 491528 | tf_op jit(solution)/shard_map/ppermute | solution.py:330
  13.2 0.9 copy-start.1
  70.9 3.3 %collective-permute-start.2 = (f32[320,128]{1,0:T(8,128)S(1)}, f32[320,128]{1,0:T(8,128)S(1)}, u32[]{:S(2)}, u32[]{:S(2)}) collective-permute-start(f32[320,128]{1,0:T(8,128)S(1)} %reduce_sum.9), channel_id=1, source_target_pairs={{0,4},{4,0},{8,12},{12,8},{1,5},{5,1},{9,13},{13,9},{2,6},{6,2},{1... | collective-permute-start | bytes 491528 | tf_op jit(solution)/shard_map/ppermute | solution.py:337
  74.2 8.1 %collective-permute-start.3 = (f32[320,128]{1,0:T(8,128)S(1)}, f32[320,128]{1,0:T(8,128)S(1)}, u32[]{:S(2)}, u32[]{:S(2)}) collective-permute-start(f32[320,128]{1,0:T(8,128)S(1)} %add_multiply_fusion), channel_id=1, source_target_pairs={{0,8},{4,12},{8,0},{12,4},{1,9},{5,13},{9,1},{13,5},{2,10},{6,14},... | collective-permute-start | bytes 491528 | tf_op jit(solution)/shard_map/ppermute | solution.py:337

commit v4 on v3

--- a/solution.py
+++ b/solution.py
@@ -51,7 +51,7 @@
         cols[slot] = block
         acc[slot] = jnp.zeros((slices, CS), jnp.float32)
     for c in range(own):
-        across[c + H] = pos[c]
+        across[c + H] = pos[c, :3]
     cols[last] = jnp.zeros((slices, CS), jnp.bfloat16)
     along[last] = jnp.zeros((CS, 384), jnp.float32)
     across[last] = jnp.zeros((3, CS), jnp.float32)
@@ -233,6 +233,7 @@
         upper[m, half:, :half] = jnp.zeros((half, half), jnp.float32)
     rowid = lax.broadcasted_iota(jnp.int32, (8, 128), 0)
     spread = lambda row: jnp.broadcast_to(row, (8, 128))
+    blank = upper[0, half : half + 8, :half]
     for j0 in range(0, n, PANEL):
         lane0 = 0 if j0 < half else half
         width = (n - lane0) // 128
@@ -244,7 +245,7 @@
             )
             at = j0 - lane0
             cols.append(
-                [[spread(block[8 * h : 8 * h + 8, at + c : at + c + 1]) for h in range(2)] for c in range(PANEL)]
+                [[spread(block[8 * h : 8 * h + 8, at + c : at + c + 1]) + blank for h in range(2)] for c in range(PANEL)]
             )
             scale.append([jnp.zeros((8, 128), jnp.float32) for h in range(2)])
         for q in range(PANEL):
@@ -328,7 +329,7 @@
     backward = [(i + 1, i) for i in range(count - 1)]
     low = lax.ppermute(edge(positions[:, -margin:], sketch[:, -margin:]), clus, forward)
     high = lax.ppermute(edge(positions[:, :margin], sketch[:, :margin]), clus, backward)
-    by_cluster = positions.reshape(3, -1, CS).transpose(1, 0, 2)
+    by_cluster = jnp.pad(positions, ((0, 1), (0, 0))).reshape(4, -1, CS).transpose(1, 0, 2)
     image, rounded = near_field(by_cluster, sketch, low, high, near, shares)
     traded = lax.all_to_all(rounded, "sk", split_axis=0, concat_axis=0, tiled=True)
     shared = partial_gram(traded, 1.0 / rows, shares)

time: 94 us -> 91.8 us (0.977)
  the two profiles are of different devices: /device:TPU:288 before, /device:TPU:100 now
where the time goes in v4:
time: 91.8 us; the launch traced here: 91.3 us
  blocking collectives  34.4 us (37%)
  Pallas kernels  34.3 us (37%)
  starting transfers between devices  9.58 us (10%)
  waiting for transfers between devices  8.49 us (9%)
  local copies, waits for them, and re-layouts  2.79 us (3%)
  other arithmetic  1.02 us (1%)
    pallas_call x1, Pallas kernels, near_field(): pl.pallas_call(near_field_kernel, out_shape=(jax.ShapeDtypeStruct((slices...  23.2 us
    all_to_all x1, blocking collectives, on_device(): lax.all_to_all(rounded, 'sk', split_axis=0, concat_axis=0, tiled=True)  20.6 us
    all_to_all x1, blocking collectives, on_device(): lax.all_to_all(shared, 'sk', split_axis=0, concat_axis=0, tiled=True)  13.8 us
    pallas_call x1, Pallas kernels, cholesky(): pl.pallas_call(cholesky_kernel, out_shape=(jax.ShapeDtypeStruct((wide, 2...  10.5 us
    ppermute x2, waiting for transfers between devices, on_device(): lax.ppermute(value, 'child', [(i, i ^ d) for i in range(FAMILY)])  7.39 us
    ppermute x2, starting transfers between devices, on_device(): lax.ppermute(value, 'child', [(i, i ^ d) for i in range(FAMILY)])  4.02 us
    ppermute x1, starting transfers between devices, on_device(): lax.ppermute(edge(positions[:, :margin], sketch[:, :margin]), clus, backw...  3.64 us
    ppermute x1, starting transfers between devices, on_device(): lax.ppermute(edge(positions[:, -margin:], sketch[:, -margin:]), clus, for...  1.92 us
  transfers between devices with their start and end apart: 4, of which 3 were waited for; matrix products, arithmetic and copies ran while one was open for 2% of the time, Pallas kernels for 0%

profile of v4, /device:TPU:100, one launch (start us, length us, event | category | flops | bytes accessed | tf_op | source)
XLA Modules:
  0.0 91.3 jit_solution(16141913861111841426)
XLA Ops:
  0.6 0.0 copy-start
  0.6 0.8 fusion.8
  1.6 1.0 %fusion.12 = (bf16[64,1024]{1,0:T(8,128)(2,1)S(1)}, bf16[64,1024]{1,0:T(8,128)(2,1)S(1)}) fusion(bf16[64,8192]{1,0:T(8,128)(2,1)} %sk.1), kind=kLoop, calls=%fused_computation.26 | loop fusion | bytes 524288 | tf_op jit(solution)/shard_map/slice | solution.py:331
  2.6 1.9 %collective-permute-start = (bf16[80,1024]{1,0:T(8,128)(2,1)S(1)}, bf16[80,1024]{1,0:T(8,128)(2,1)S(1)}, u32[]{:S(2)}, u32[]{:S(2)}) collective-permute-start(bf16[80,1024]{1,0:T(8,128)(2,1)S(1)} %fusion.2), channel_id=1, source_target_pairs={{0,4},{4,8},{8,12},{12,16},{16,20},{20,24},{24,28},{28,32},{32,36}... | collective-permute-start | bytes 491528 | tf_op jit(solution)/shard_map/ppermute | solution.py:330
  4.6 3.6 %collective-permute-start.1 = (bf16[80,1024]{1,0:T(8,128)(2,1)S(1)}, bf16[80,1024]{1,0:T(8,128)(2,1)S(1)}, u32[]{:S(2)}, u32[]{:S(2)}) collective-permute-start(bf16[80,1024]{1,0:T(8,128)(2,1)S(1)} %fusion.3), channel_id=1, source_target_pairs={{4,0},{8,4},{12,8},{16,12},{20,16},{24,20},{28,24},{32,28},{36,32}... | collective-permute-start | bytes 491528 | tf_op jit(solution)/shard_map/ppermute | solution.py:331
  8.3 0.9 %pad.11 = f32[4,8192]{1,0:T(4,128)S(1)} pad(f32[3,8192]{1,0:T(4,128)} %param.3, f32[]{:T(128)} %constant.4.clone.1), padding=0_1x0_0 | pad | bytes 229380 | tf_op jit(solution)/shard_map/jit(_pad)/pad | solution.py:332
  9.2 0.8 copy.9.near_far
  10.0 0.0 collective-permute-done.low
  10.0 1.1 %collective-permute-done.1.high = bf16[80,1024]{1,0:T(8,128)(2,1)S(1)} collective-permute-done((bf16[80,1024]{1,0:T(8,128)(2,1)S(1)}, bf16[80,1024]{1,0:T(8,128)(2,1)S(1)}, u32[]{:S(2)}, u32[]{:S(2)}) %collective-permute-start.1) | collective-permute-done | bytes 163872 | tf_op jit(solution)/shard_map/ppermute | solution.py:331
  11.1 0.0 copy-done
  11.1 23.2 %near_field.1 = (f32[64,8192]{1,0:T(8,128)}, bf16[4,64,2048]{2,1,0:T(8,128)(2,1)S(1)}) custom-call(f32[32,4,256]{2,1,0:T(4,128)S(1)} %bitcast.23, bf16[64,8192]{1,0:T(8,128)(2,1)S(1)} %copy-done, bf16[80,1024]{1,0:T(8,128)(2,1)S(1)} %collective-permute-done.low, bf16[80,1024]{1,0:T(8,128)(2,1)S(1)} %collective-permute-done.1.high, s32[32,9]{1,0:T(8,128)S(1)} %copy.9.near_far), custom_call_target="tpu_custom_call" | custom-call | tf_op jit(solution)/shard_map/near_field/pallas_call | solution.py:155
  34.3 20.6 %all_to_all.10.points = bf16[4,64,2048]{2,1,0:T(8,128)(2,1)S(1)} all-to-all(bf16[4,64,2048]{2,1,0:T(8,128)(2,1)S(1)} %get-tuple-element.10), channel_id=1, replica_groups=mesh['tree'=32,'child'=4,'sk'=4] {'sk'}, dimensions={0} | all-to-all | bytes 2097152 | tf_op jit(solution)/shard_map/all_to_all | solution.py:334
  54.9 0.5 partial_gram.1
  55.4 13.8 %all_to_all.11 = f32[4,320,128]{2,1,0:T(8,128)S(1)} all-to-all(f32[4,320,128]{2,1,0:T(8,128)S(1)} %partial_gram.1), channel_id=1, replica_groups=mesh['tree'=32,'child'=4,'sk'=4] {'sk'}, dimensions={0} | all-to-all | bytes 1310720 | tf_op jit(solution)/shard_map/all_to_all | solution.py:336
  69.3 1.9 %collective-permute-start.2 = (f32[320,128]{1,0:T(8,128)S(1)}, f32[320,128]{1,0:T(8,128)S(1)}, u32[]{:S(2)}, u32[]{:S(2)}) collective-permute-start(f32[320,128]{1,0:T(8,128)S(1)} %reduce_sum.9), channel_id=1, source_target_pairs={{0,4},{4,0},{8,12},{12,8},{1,5},{5,1},{9,13},{13,9},{2,6},{6,2},{1... | collective-permute-start | bytes 491528 | tf_op jit(solution)/shard_map/ppermute | solution.py:338
  71.2 1.4 %collective-permute-done.2 = f32[320,128]{1,0:T(8,128)S(1)} collective-permute-done((f32[320,128]{1,0:T(8,128)S(1)}, f32[320,128]{1,0:T(8,128)S(1)}, u32[]{:S(2)}, u32[]{:S(2)}) %collective-permute-start.2) | collective-permute-done | bytes 163872 | tf_op jit(solution)/shard_map/ppermute | solution.py:338
  72.6 2.1 %collective-permute-start.3 = (f32[320,128]{1,0:T(8,128)S(1)}, f32[320,128]{1,0:T(8,128)S(1)}, u32[]{:S(2)}, u32[]{:S(2)}) collective-permute-start(f32[320,128]{1,0:T(8,128)S(1)} %add_multiply_fusion), channel_id=1, source_target_pairs={{0,8},{4,12},{8,0},{12,4},{1,9},{5,13},{9,1},{13,5},{2,10},{6,14},... | collective-permute-start | bytes 491528 | tf_op jit(solution)/shard_map/ppermute | solution.py:338
  74.7 6.0 %collective-permute-done.3 = f32[320,128]{1,0:T(8,128)S(1)} collective-permute-done((f32[320,128]{1,0:T(8,128)S(1)}, f32[320,128]{1,0:T(8,128)S(1)}, u32[]{:S(2)}, u32[]{:S(2)}) %collective-permute-start.3) | collective-permute-done | bytes 163872 | tf_op jit(solution)/shard_map/ppermute | solution.py:338
  80.8 10.5 %cholesky.1 = (f32[64,256]{1,0:T(8,128)}, f32[64,256]{1,0:T(8,128)}, f32[64,256]{1,0:T(8,128)}) custom-call(s32[1]{0:T(128)} %bitcast.8.place, f32[3,320,128]{2,1,0:T(8,128)S(1)} %pad_maximum_fusion.grams), custom_call_target="tpu_custom_call" | custom-call | tf_op jit(solution)/shard_map/cholesky/pallas_call | solution.py:303
  (11 shorter events, 0.3 us)
Async XLA Ops:
  0.6 10.5 %copy-start = (bf16[64,8192]{1,0:T(8,128)(2,1)S(1)}, bf16[64,8192]{1,0:T(8,128)(2,1)}, u32[]{:S(2)}) copy-start(bf16[64,8192]{1,0:T(8,128)(2,1)} %sk.1) | copy-start | bytes 3145732
  2.6 7.4 %collective-permute-start = (bf16[80,1024]{1,0:T(8,128)(2,1)S(1)}, bf16[80,1024]{1,0:T(8,128)(2,1)S(1)}, u32[]{:S(2)}, u32[]{:S(2)}) collective-permute-start(bf16[80,1024]{1,0:T(8,128)(2,1)S(1)} %fusion.2), channel_id=1, source_target_pairs={{0,4},{4,8},{8,12},{12,16},{16,20},{20,24},{24,28},{28,32},{32,36}... | collective-permute-start | bytes 491528 | tf_op jit(solution)/shard_map/ppermute | solution.py:330
  4.6 6.5 %collective-permute-start.1 = (bf16[80,1024]{1,0:T(8,128)(2,1)S(1)}, bf16[80,1024]{1,0:T(8,128)(2,1)S(1)}, u32[]{:S(2)}, u32[]{:S(2)}) collective-permute-start(bf16[80,1024]{1,0:T(8,128)(2,1)S(1)} %fusion.3), channel_id=1, source_target_pairs={{4,0},{8,4},{12,8},{16,12},{20,16},{24,20},{28,24},{32,28},{36,32}... | collective-permute-start | bytes 491528 | tf_op jit(solution)/shard_map/ppermute | solution.py:331
  69.3 3.3 %collective-permute-start.2 = (f32[320,128]{1,0:T(8,128)S(1)}, f32[320,128]{1,0:T(8,128)S(1)}, u32[]{:S(2)}, u32[]{:S(2)}) collective-permute-start(f32[320,128]{1,0:T(8,128)S(1)} %reduce_sum.9), channel_id=1, source_target_pairs={{0,4},{4,0},{8,12},{12,8},{1,5},{5,1},{9,13},{13,9},{2,6},{6,2},{1... | collective-permute-start | bytes 491528 | tf_op jit(solution)/shard_map/ppermute | solution.py:338
  72.6 8.1 %collective-permute-start.3 = (f32[320,128]{1,0:T(8,128)S(1)}, f32[320,128]{1,0:T(8,128)S(1)}, u32[]{:S(2)}, u32[]{:S(2)}) collective-permute-start(f32[320,128]{1,0:T(8,128)S(1)} %add_multiply_fusion), channel_id=1, source_target_pairs={{0,8},{4,12},{8,0},{12,4},{1,9},{5,13},{9,1},{13,5},{2,10},{6,14},... | collective-permute-start | bytes 491528 | tf_op jit(solution)/shard_map/ppermute | solution.py:338

commit v5 on v4

--- a/solution.py
+++ b/solution.py
@@ -14,7 +14,7 @@
 RATE = math.sqrt(3.0) / 0.3
 NUGGET = 1.0
 FAMILY = 4
-UNROLL = 4
+UNROLL = 6
 PANEL = 16
 SHIFT = 64
 
@@ -166,7 +166,7 @@
             pltpu.VMEM((slots, CS, 3 * 128), jnp.float32),
             pltpu.VMEM((slots, slices, CS), jnp.bfloat16),
             pltpu.VMEM((slots, slices, CS), jnp.float32),
-            pltpu.VMEM((UNROLL, CS, CS), jnp.bfloat16),
+            pltpu.VMEM((max(UNROLL, 4), CS, CS), jnp.bfloat16),
             pltpu.SMEM((slots * H + 4 * UNROLL,), jnp.int32),
             pltpu.SemaphoreType.DMA,
         ],

time: 91.8 us -> 92 us (level)
  the two profiles are of different devices: /device:TPU:100 before, /device:TPU:326 now
where the time goes in v5:
time: 92 us; the launch traced here: 90.4 us
  blocking collectives  34.2 us (37%)
  Pallas kernels  33.5 us (36%)
  starting transfers between devices  9.58 us (10%)
  waiting for transfers between devices  8.49 us (9%)
  local copies, waits for them, and re-layouts  2.79 us (3%)
  other arithmetic  1.02 us (1%)
    pallas_call x1, Pallas kernels, near_field(): pl.pallas_call(near_field_kernel, out_shape=(jax.ShapeDtypeStruct((slices...  22.4 us
    all_to_all x1, blocking collectives, on_device(): lax.all_to_all(rounded, 'sk', split_axis=0, concat_axis=0, tiled=True)  20.6 us
    all_to_all x1, blocking collectives, on_device(): lax.all_to_all(shared, 'sk', split_axis=0, concat_axis=0, tiled=True)  13.6 us
    pallas_call x1, Pallas kernels, cholesky(): pl.pallas_call(cholesky_kernel, out_shape=(jax.ShapeDtypeStruct((wide, 2...  10.5 us
    ppermute x2, waiting for transfers between devices, on_device(): lax.ppermute(value, 'child', [(i, i ^ d) for i in range(FAMILY)])  7.39 us
    ppermute x2, starting transfers between devices, on_device(): lax.ppermute(value, 'child', [(i, i ^ d) for i in range(FAMILY)])  4.02 us
    ppermute x1, starting transfers between devices, on_device(): lax.ppermute(edge(positions[:, :margin], sketch[:, :margin]), clus, backw...  3.64 us
    ppermute x1, starting transfers between devices, on_device(): lax.ppermute(edge(positions[:, -margin:], sketch[:, -margin:]), clus, for...  1.92 us
  transfers between devices with their start and end apart: 4, of which 3 were waited for; matrix products, arithmetic and copies ran while one was open for 2% of the time, Pallas kernels for 0%

profile of v5, /device:TPU:326, one launch (start us, length us, event | category | flops | bytes accessed | tf_op | source)
XLA Modules:
  0.0 90.4 jit_solution(1585004736559519940)
XLA Ops:
  0.6 0.0 copy-start
  0.6 0.8 fusion.8
  1.6 1.0 %fusion.12 = (bf16[64,1024]{1,0:T(8,128)(2,1)S(1)}, bf16[64,1024]{1,0:T(8,128)(2,1)S(1)}) fusion(bf16[64,8192]{1,0:T(8,128)(2,1)} %sk.1), kind=kLoop, calls=%fused_computation.26 | loop fusion | bytes 524288 | tf_op jit(solution)/shard_map/slice | solution.py:331
  2.6 1.9 %collective-permute-start = (bf16[80,1024]{1,0:T(8,128)(2,1)S(1)}, bf16[80,1024]{1,0:T(8,128)(2,1)S(1)}, u32[]{:S(2)}, u32[]{:S(2)}) collective-permute-start(bf16[80,1024]{1,0:T(8,128)(2,1)S(1)} %fusion.2), channel_id=1, source_target_pairs={{0,4},{4,8},{8,12},{12,16},{16,20},{20,24},{24,28},{28,32},{32,36}... | collective-permute-start | bytes 491528 | tf_op jit(solution)/shard_map/ppermute | solution.py:330
  4.6 3.6 %collective-permute-start.1 = (bf16[80,1024]{1,0:T(8,128)(2,1)S(1)}, bf16[80,1024]{1,0:T(8,128)(2,1)S(1)}, u32[]{:S(2)}, u32[]{:S(2)}) collective-permute-start(bf16[80,1024]{1,0:T(8,128)(2,1)S(1)} %fusion.3), channel_id=1, source_target_pairs={{4,0},{8,4},{12,8},{16,12},{20,16},{24,20},{28,24},{32,28},{36,32}... | collective-permute-start | bytes 491528 | tf_op jit(solution)/shard_map/ppermute | solution.py:331
  8.3 0.9 %pad.11 = f32[4,8192]{1,0:T(4,128)S(1)} pad(f32[3,8192]{1,0:T(4,128)} %param.3, f32[]{:T(128)} %constant.4.clone.1), padding=0_1x0_0 | pad | bytes 229380 | tf_op jit(solution)/shard_map/jit(_pad)/pad | solution.py:332
  9.2 0.8 copy.9.near_far
  10.0 0.0 collective-permute-done.low
  10.0 1.1 %collective-permute-done.1.high = bf16[80,1024]{1,0:T(8,128)(2,1)S(1)} collective-permute-done((bf16[80,1024]{1,0:T(8,128)(2,1)S(1)}, bf16[80,1024]{1,0:T(8,128)(2,1)S(1)}, u32[]{:S(2)}, u32[]{:S(2)}) %collective-permute-start.1) | collective-permute-done | bytes 163872 | tf_op jit(solution)/shard_map/ppermute | solution.py:331
  11.1 0.0 copy-done
  11.1 22.4 %near_field.1 = (f32[64,8192]{1,0:T(8,128)}, bf16[4,64,2048]{2,1,0:T(8,128)(2,1)S(1)}) custom-call(f32[32,4,256]{2,1,0:T(4,128)S(1)} %bitcast.23, bf16[64,8192]{1,0:T(8,128)(2,1)S(1)} %copy-done, bf16[80,1024]{1,0:T(8,128)(2,1)S(1)} %collective-permute-done.low, bf16[80,1024]{1,0:T(8,128)(2,1)S(1)} %collective-permute-done.1.high, s32[32,9]{1,0:T(8,128)S(1)} %copy.9.near_far), custom_call_target="tpu_custom_call" | custom-call | tf_op jit(solution)/shard_map/near_field/pallas_call | solution.py:155
  33.5 20.6 %all_to_all.10.points = bf16[4,64,2048]{2,1,0:T(8,128)(2,1)S(1)} all-to-all(bf16[4,64,2048]{2,1,0:T(8,128)(2,1)S(1)} %get-tuple-element.10), channel_id=1, replica_groups=mesh['tree'=32,'child'=4,'sk'=4] {'sk'}, dimensions={0} | all-to-all | bytes 2097152 | tf_op jit(solution)/shard_map/all_to_all | solution.py:334
  54.1 0.5 partial_gram.1
  54.6 13.6 %all_to_all.11 = f32[4,320,128]{2,1,0:T(8,128)S(1)} all-to-all(f32[4,320,128]{2,1,0:T(8,128)S(1)} %partial_gram.1), channel_id=1, replica_groups=mesh['tree'=32,'child'=4,'sk'=4] {'sk'}, dimensions={0} | all-to-all | bytes 1310720 | tf_op jit(solution)/shard_map/all_to_all | solution.py:336
  68.3 1.9 %collective-permute-start.2 = (f32[320,128]{1,0:T(8,128)S(1)}, f32[320,128]{1,0:T(8,128)S(1)}, u32[]{:S(2)}, u32[]{:S(2)}) collective-permute-start(f32[320,128]{1,0:T(8,128)S(1)} %reduce_sum.9), channel_id=1, source_target_pairs={{0,4},{4,0},{8,12},{12,8},{1,5},{5,1},{9,13},{13,9},{2,6},{6,2},{1... | collective-permute-start | bytes 491528 | tf_op jit(solution)/shard_map/ppermute | solution.py:338
  70.3 1.4 %collective-permute-done.2 = f32[320,128]{1,0:T(8,128)S(1)} collective-permute-done((f32[320,128]{1,0:T(8,128)S(1)}, f32[320,128]{1,0:T(8,128)S(1)}, u32[]{:S(2)}, u32[]{:S(2)}) %collective-permute-start.2) | collective-permute-done | bytes 163872 | tf_op jit(solution)/shard_map/ppermute | solution.py:338
  71.6 2.1 %collective-permute-start.3 = (f32[320,128]{1,0:T(8,128)S(1)}, f32[320,128]{1,0:T(8,128)S(1)}, u32[]{:S(2)}, u32[]{:S(2)}) collective-permute-start(f32[320,128]{1,0:T(8,128)S(1)} %add_multiply_fusion), channel_id=1, source_target_pairs={{0,8},{4,12},{8,0},{12,4},{1,9},{5,13},{9,1},{13,5},{2,10},{6,14},... | collective-permute-start | bytes 491528 | tf_op jit(solution)/shard_map/ppermute | solution.py:338
  73.8 6.0 %collective-permute-done.3 = f32[320,128]{1,0:T(8,128)S(1)} collective-permute-done((f32[320,128]{1,0:T(8,128)S(1)}, f32[320,128]{1,0:T(8,128)S(1)}, u32[]{:S(2)}, u32[]{:S(2)}) %collective-permute-start.3) | collective-permute-done | bytes 163872 | tf_op jit(solution)/shard_map/ppermute | solution.py:338
  79.9 10.5 %cholesky.1 = (f32[64,256]{1,0:T(8,128)}, f32[64,256]{1,0:T(8,128)}, f32[64,256]{1,0:T(8,128)}) custom-call(s32[1]{0:T(128)} %bitcast.8.place, f32[3,320,128]{2,1,0:T(8,128)S(1)} %pad_maximum_fusion.grams), custom_call_target="tpu_custom_call" | custom-call | tf_op jit(solution)/shard_map/cholesky/pallas_call | solution.py:303
  (11 shorter events, 0.3 us)
Async XLA Ops:
  0.6 10.5 %copy-start = (bf16[64,8192]{1,0:T(8,128)(2,1)S(1)}, bf16[64,8192]{1,0:T(8,128)(2,1)}, u32[]{:S(2)}) copy-start(bf16[64,8192]{1,0:T(8,128)(2,1)} %sk.1) | copy-start | bytes 3145732
  2.6 7.4 %collective-permute-start = (bf16[80,1024]{1,0:T(8,128)(2,1)S(1)}, bf16[80,1024]{1,0:T(8,128)(2,1)S(1)}, u32[]{:S(2)}, u32[]{:S(2)}) collective-permute-start(bf16[80,1024]{1,0:T(8,128)(2,1)S(1)} %fusion.2), channel_id=1, source_target_pairs={{0,4},{4,8},{8,12},{12,16},{16,20},{20,24},{24,28},{28,32},{32,36}... | collective-permute-start | bytes 491528 | tf_op jit(solution)/shard_map/ppermute | solution.py:330
  4.6 6.5 %collective-permute-start.1 = (bf16[80,1024]{1,0:T(8,128)(2,1)S(1)}, bf16[80,1024]{1,0:T(8,128)(2,1)S(1)}, u32[]{:S(2)}, u32[]{:S(2)}) collective-permute-start(bf16[80,1024]{1,0:T(8,128)(2,1)S(1)} %fusion.3), channel_id=1, source_target_pairs={{4,0},{8,4},{12,8},{16,12},{20,16},{24,20},{28,24},{32,28},{36,32}... | collective-permute-start | bytes 491528 | tf_op jit(solution)/shard_map/ppermute | solution.py:331
  68.3 3.3 %collective-permute-start.2 = (f32[320,128]{1,0:T(8,128)S(1)}, f32[320,128]{1,0:T(8,128)S(1)}, u32[]{:S(2)}, u32[]{:S(2)}) collective-permute-start(f32[320,128]{1,0:T(8,128)S(1)} %reduce_sum.9), channel_id=1, source_target_pairs={{0,4},{4,0},{8,12},{12,8},{1,5},{5,1},{9,13},{13,9},{2,6},{6,2},{1... | collective-permute-start | bytes 491528 | tf_op jit(solution)/shard_map/ppermute | solution.py:338
  71.6 8.1 %collective-permute-start.3 = (f32[320,128]{1,0:T(8,128)S(1)}, f32[320,128]{1,0:T(8,128)S(1)}, u32[]{:S(2)}, u32[]{:S(2)}) collective-permute-start(f32[320,128]{1,0:T(8,128)S(1)} %add_multiply_fusion), channel_id=1, source_target_pairs={{0,8},{4,12},{8,0},{12,4},{1,9},{5,13},{9,1},{13,5},{2,10},{6,14},... | collective-permute-start | bytes 491528 | tf_op jit(solution)/shard_map/ppermute | solution.py:338
